TPU v7x, 32 devices: a whole 2x2x4 slice. The times are simulated.
32 devices in a mesh: section: 4 (over z), seq: 2 (over y), tp: 4 (over x, core).
Axes of the slice: x: 2, y: 2, z: 4, core: 2. Of those that a mesh axis runs over, the one named last changes fastest.
Arguments:
- text_rows: bfloat16 [128, 8192], P(None, ('seq', 'tp')), may hold values from -6 to 6
- image_rows: bfloat16 [128, 8192], P(('seq', 'tp')), may hold values from -6 to 6
- image_target: int32 [128], P(('seq', 'tp')), may hold values from -1 to 63, as said below
- norm_gain: bfloat16 [4, 8192], P('section', ('seq', 'tp')), may hold values from 0.099609375 to 1.8984375
- q_weight: bfloat16 [4, 8192, 1024], P('section', None, ('seq', 'tp')), may hold values from -0.0625 to 0.0625
- q_bias: bfloat16 [4, 1024], P('section', ('seq', 'tp')), may hold values from -3 to 3
- kv_weight: bfloat16 [4, 8192, 4, 256], P('section', None, 'tp'), may hold values from -0.0625 to 0.0625
- kv_bias: bfloat16 [4, 4, 256], P('section', 'tp'), may hold values from -3 to 3
- out_weight: bfloat16 [4, 1024, 8192], P('section', None, ('seq', 'tp')), may hold values from -0.1875 to 0.1875
Outputs:
- layer_outputs: bfloat16 [4, 128, 8192], P('section', None, ('seq', 'tp'))
Inputs may be any that keep to these rules, and one draw needn't show every extreme that they name: `image_target`: in each micro-batch's 64 entries exactly 56 are token positions, all different, and the others are -1.
All inputs are finite; a program needn't handle non-finite values.
Results may differ from a plain program's by a relative error of at most 0.015.
Values may be sent and summed in bfloat16 or wider, within the bound.
A program may use at most 64 MiB of HBM per device.

v0:
```python
import math

import jax
import jax.numpy as jnp
from jax import lax
from jax.sharding import PartitionSpec as P

MICRO = 2


EPS = 1e-06
THETA = 1000000.0


def from_behind(block, axis, distance):
    devices = range(lax.axis_size(axis))
    route = [(i - distance, i) for i in devices if i - distance in devices]
    return lax.ppermute(block, axis, route)


def rotate(values, cosine, sine_tab):
    half_size = values.shape[-1] // 2
    turned = jnp.concatenate([-values[..., half_size:], values[..., :half_size]], axis=-1)
    return values * cosine + turned * sine_tab


def tables(positions, head_size):
    half_size = head_size // 2
    frequency = THETA ** (-jnp.arange(half_size, dtype=jnp.float32) * 2.0 / head_size)
    angles = positions.astype(jnp.float32)[:, None] * frequency[None, :]
    cosine = jnp.concatenate([jnp.cos(angles), jnp.cos(angles)], axis=-1)
    sine_tab = jnp.concatenate([jnp.sin(angles), jnp.sin(angles)], axis=-1)
    return (cosine, sine_tab)


def add_rows(piece, weight):
    return jnp.dot(piece, weight, preferred_element_type=jnp.float32)


def per_device(
    text_rows, image_rows, image_target, norm_gain, q_weight, q_bias, kv_weight, kv_bias, out_weight
):
    members = lax.axis_size(("seq", "tp"))
    member_index = lax.axis_index(("seq", "tp"))
    sections = lax.axis_size("section")
    section_index = lax.axis_index("section")
    col_width = text_rows.shape[1]
    feat_width = col_width * members
    head_size = q_weight.shape[2]
    tok_count = text_rows.shape[0] // MICRO
    pictures_all, targets = (
        lax.all_gather(image_rows, ("seq", "tp"), axis=0, tiled=True),
        lax.all_gather(image_target, ("seq", "tp"), axis=0, tiled=True),
    )
    pictures = lax.dynamic_slice_in_dim(pictures_all, member_index * col_width, col_width, 1)
    slot_count = targets.shape[0] // MICRO
    slot_grid = targets.reshape(MICRO, slot_count)
    positions = jnp.arange(tok_count, dtype=jnp.int32)
    matched = slot_grid[:, None, :] == positions[None, :, None]
    placed = jnp.einsum(
        "mps,msd->mpd",
        matched.astype(jnp.bfloat16),
        pictures.reshape(MICRO, slot_count, col_width),
        preferred_element_type=jnp.float32,
    )
    is_image = jnp.any(matched, axis=-1)
    text_grid = text_rows.reshape(MICRO, tok_count, col_width).astype(jnp.float32)
    embedded = jnp.where(is_image[..., None], placed, text_grid).astype(jnp.bfloat16)
    joint_weight = jnp.concatenate(
        [q_weight[0], kv_weight[0].reshape(feat_width, 2 * head_size)], axis=1
    )
    joint_bias = jnp.concatenate([q_bias[0], kv_bias[0].reshape(2 * head_size)]).astype(jnp.float32)
    output_weight = out_weight[0]
    cosine, sine_tab = tables(positions, head_size)
    causal = positions[:, None] >= positions[None, :]

    def fold_output(piece):
        return add_rows(piece, output_weight)

    def apply_layer(current):
        residual = current.astype(jnp.float32)
        whole_rows, whole_gain = (
            lax.all_gather(current, ("seq", "tp"), axis=1, tiled=True),
            lax.all_gather(norm_gain[0], ("seq", "tp"), axis=0, tiled=True),
        )
        whole_res = whole_rows.astype(jnp.float32)
        inv_rms = lax.rsqrt(jnp.mean(whole_res * whole_res, axis=1, keepdims=True) + EPS)
        normed = (whole_res * inv_rms * whole_gain.astype(jnp.float32)).astype(jnp.bfloat16)
        projected = jnp.dot(normed, joint_weight, preferred_element_type=jnp.float32)
        biased = projected + joint_bias
        queries = rotate(biased[:, :head_size], cosine, sine_tab).astype(jnp.bfloat16)
        key_rows = rotate(biased[:, head_size : 2 * head_size], cosine, sine_tab).astype(
            jnp.bfloat16
        )
        value_rows = biased[:, 2 * head_size :].astype(jnp.bfloat16)
        scores = lax.dot_general(
            queries, key_rows, (((1,), (1,)), ((), ())), preferred_element_type=jnp.float32
        )
        scores = jnp.where(causal, scores / math.sqrt(head_size), -1e30)
        row_max = jnp.max(scores, axis=1, keepdims=True)
        expo = jnp.exp(scores - row_max)
        weights_bf = (expo / jnp.sum(expo, axis=1, keepdims=True)).astype(jnp.bfloat16)
        context = jnp.dot(weights_bf, value_rows, preferred_element_type=jnp.float32).astype(
            jnp.bfloat16
        )
        update = fold_output(lax.all_gather(context, ("seq", "tp"), axis=1, tiled=True))
        return (residual + update).astype(jnp.bfloat16)

    def advance(step_index, carry):
        stored, inflow = carry
        first_mb = lax.dynamic_index_in_dim(
            embedded, jnp.minimum(step_index, MICRO - 1), 0, keepdims=False
        )
        current = jnp.where(section_index == 0, first_mb, inflow)
        result = apply_layer(current)
        own_mb = step_index - section_index
        valid = jnp.logical_and(own_mb >= 0, own_mb < MICRO)
        slot_index = jnp.clip(own_mb, 0, MICRO - 1)
        previous = lax.dynamic_index_in_dim(stored, slot_index, 0, keepdims=False)
        stored = lax.dynamic_update_index_in_dim(
            stored, jnp.where(valid, result, previous), slot_index, 0
        )
        inflow = from_behind(result, "section", 1)
        return (stored, inflow)

    step_total = sections + MICRO - 1
    stored_init = jnp.zeros((MICRO, tok_count, col_width), jnp.bfloat16)
    inflow_init = jnp.zeros((tok_count, col_width), jnp.bfloat16)
    stored, inflow = lax.fori_loop(0, step_total, advance, (stored_init, inflow_init))
    return stored.reshape(1, MICRO * tok_count, col_width)


def solution(mesh):
    in_specs = (
        P(None, ("seq", "tp")),
        P(("seq", "tp"), None),
        P(("seq", "tp")),
        P("section", ("seq", "tp")),
        P("section", None, ("seq", "tp")),
        P("section", ("seq", "tp")),
        P("section", None, "tp", None),
        P("section", "tp", None),
        P("section", None, ("seq", "tp")),
    )
    out_specs = P("section", None, ("seq", "tp"))
    return jax.shard_map(
        per_device, mesh=mesh, in_specs=in_specs, out_specs=out_specs, check_vma=False
    )
```

profile of v0, /device:TPU:25, one launch (start us, length us, event | category | flops | bytes accessed | tf_op | source)
XLA Modules:
  0.0 295.2 jit_solution(11559647502874007037)
XLA Ops:
  6.5 0.7 all-gather.7.cloned.1.call-update
  7.3 1.2 dynamic-slice
  9.2 0.9 dynamic-update-slice
  10.0 6.5 %all-reduce = s32[128]{0:T(128)S(1)} all-reduce(s32[128]{0:T(128)S(1)} %dynamic-update-slice), channel_id=1, replica_groups=mesh['section'=4,'seq'=2,'tp'=4] {'seq','tp'}, use_global_device_ids=true, to_apply=%add | all-reduce | flops 128 | bytes 1024
  16.6 0.7 reduce
  18.4 6.5 %pad_maximum_fusion = bf16[8192,384]{1,0:T(8,128)(2,1)} fusion(bf16[8192,256]{1,0:T(8,128)(2,1)} %bitcast.37, bf16[8192,128]{1,0:T(8,128)(2,1)} %bitcast.39), kind=kLoop, calls=%fused_computation.37 | loop fusion | flops 12582912 | bytes 12582912 | tf_op jit(solution)/shard_map/concatenate | solution.py:69
  24.9 13.7 %all-gather.7.cloned.1.call-done = bf16[128,8192]{1,0:T(8,128)(2,1)} async-done(((bf16[16,8192]{1,0:T(8,128)(2,1)}), bf16[128,8192]{1,0:T(8,128)(2,1)}) %all-gather.7.cloned.1.call-update) | async-done | bytes 2097168 | tf_op jit(solution)/shard_map/all_gather | solution.py:52
  38.6 1.0 constant_dynamic-slice_fusion.1
  39.9 247.8 %while.17 = (s32[]{:T(128)}, bf16[2,64,1024]{2,1,0:T(8,128)(2,1)S(1)}, bf16[64,1024]{1,0:T(8,128)(2,1)S(1)}, s32[]{:T(128)}, pred[]{:T(512)}, /*index=5*/bf16[2,...) while((s32[]{:T(128)}, ...), condition=%wide.region_5.6_spmd.clone, body=%wide.region_1.5_spmd.clone.sunk | while | flops 543133632 | bytes 17291884 | solution.py:129
  39.9 0.7 bitcast_select_fusion.3
  40.6 9.1 %all-gather.3 = bf16[1,8192]{1,0:T(2,128)(2,1)S(1)} all-gather(bf16[1,1024]{1,0:T(2,128)(2,1)S(1)} %get-tuple-element.445), channel_id=2, replica_groups=mesh['section'=4,'seq'=2,'tp'=4] {'seq','tp'}, dimensions={1}, use_global_device_ids=true | all-gather | bytes 18432 | tf_op jit(solution)/shard_map/while/body/eval_jaxpr/all_gather | solution.py:84
  49.8 16.4 %all-gather.9.cloned.1.call-done = bf16[64,8192]{1,0:T(8,128)(2,1)} async-done(((bf16[64,1024]{1,0:T(8,128)(2,1)}), bf16[64,8192]{1,0:T(8,128)(2,1)}) %all-gather.9.cloned.1.call-update) | async-done | bytes 1048592 | tf_op jit(solution)/shard_map/while/body/eval_jaxpr/all_gather | solution.py:83
  66.2 1.5 fusion.39
  67.7 4.3 %convolution_add_fusion.3 = f32[64,384]{1,0:T(8,128)S(1)} fusion(bf16[8192,384]{1,0:T(8,128)(2,1)} %get-tuple-element.446, bf16[64,8192]{1,0:T(8,128)(2,1)} %all-gather.9.cloned.1.call-done, f32[8192]{0:T(1024)S(1)} %bitcast.38, f32[64]{0:T(128)S(1)} %add_rsqrt_fusion.2, f32[384]{0:T(512)S(1)} %get-tuple-element.447), kind=kOutput, calls=%fused_computation.8.clone.1 | convolution fusion | flops 404774912 | bytes 7472896 | tf_op jit(solution)/shard_map/while/body/eval_jaxpr/dot_general | solution.py:89
  72.6 9.1 %all_gather.37 = bf16[64,1024]{1,0:T(8,128)(2,1)S(1)} all-gather(bf16[64,128]{1,0:T(8,128)(2,1)S(1)} %convolution_convert_fusion.2), channel_id=1, replica_groups=mesh['section'=4,'seq'=2,'tp'=4] {'seq','tp'}, dimensions={1}, use_global_device_ids=true | all-gather | bytes 147456 | tf_op jit(solution)/shard_map/while/body/eval_jaxpr/all_gather | solution.py:106
  82.2 1.3 collective-permute-start
  83.5 5.5 %collective-permute-done = bf16[64,1024]{1,0:T(8,128)(2,1)S(1)} collective-permute-done((bf16[64,1024]{1,0:T(8,128)(2,1)S(1)}, bf16[64,1024]{1,0:T(8,128)(2,1)S(1)}, u32[]{:S(2)}, u32[]{:S(2)}) %collective-permute-start) | collective-permute-done | bytes 131104 | tf_op jit(solution)/shard_map/while/body/eval_jaxpr/ppermute | solution.py:18
  89.1 0.7 bitcast_select_fusion.3
  89.8 8.9 %all-gather.3 = bf16[1,8192]{1,0:T(2,128)(2,1)S(1)} all-gather(bf16[1,1024]{1,0:T(2,128)(2,1)S(1)} %get-tuple-element.445), channel_id=2, replica_groups=mesh['section'=4,'seq'=2,'tp'=4] {'seq','tp'}, dimensions={1}, use_global_device_ids=true | all-gather | bytes 18432 | tf_op jit(solution)/shard_map/while/body/eval_jaxpr/all_gather | solution.py:84
  98.8 17.3 %all-gather.9.cloned.1.call-done = bf16[64,8192]{1,0:T(8,128)(2,1)} async-done(((bf16[64,1024]{1,0:T(8,128)(2,1)}), bf16[64,8192]{1,0:T(8,128)(2,1)}) %all-gather.9.cloned.1.call-update) | async-done | bytes 1048592 | tf_op jit(solution)/shard_map/while/body/eval_jaxpr/all_gather | solution.py:83
  116.0 1.5 fusion.39
  117.6 4.3 %convolution_add_fusion.3 = f32[64,384]{1,0:T(8,128)S(1)} fusion(bf16[8192,384]{1,0:T(8,128)(2,1)} %get-tuple-element.446, bf16[64,8192]{1,0:T(8,128)(2,1)} %all-gather.9.cloned.1.call-done, f32[8192]{0:T(1024)S(1)} %bitcast.38, f32[64]{0:T(128)S(1)} %add_rsqrt_fusion.2, f32[384]{0:T(512)S(1)} %get-tuple-element.447), kind=kOutput, calls=%fused_computation.8.clone.1 | convolution fusion | flops 404774912 | bytes 7472896 | tf_op jit(solution)/shard_map/while/body/eval_jaxpr/dot_general | solution.py:89
  122.5 9.1 %all_gather.37 = bf16[64,1024]{1,0:T(8,128)(2,1)S(1)} all-gather(bf16[64,128]{1,0:T(8,128)(2,1)S(1)} %convolution_convert_fusion.2), channel_id=1, replica_groups=mesh['section'=4,'seq'=2,'tp'=4] {'seq','tp'}, dimensions={1}, use_global_device_ids=true | all-gather | bytes 147456 | tf_op jit(solution)/shard_map/while/body/eval_jaxpr/all_gather | solution.py:106
  132.1 1.3 collective-permute-start
  133.4 5.5 %collective-permute-done = bf16[64,1024]{1,0:T(8,128)(2,1)S(1)} collective-permute-done((bf16[64,1024]{1,0:T(8,128)(2,1)S(1)}, bf16[64,1024]{1,0:T(8,128)(2,1)S(1)}, u32[]{:S(2)}, u32[]{:S(2)}) %collective-permute-start) | collective-permute-done | bytes 131104 | tf_op jit(solution)/shard_map/while/body/eval_jaxpr/ppermute | solution.py:18
  138.9 0.7 bitcast_select_fusion.3
  139.6 8.9 %all-gather.3 = bf16[1,8192]{1,0:T(2,128)(2,1)S(1)} all-gather(bf16[1,1024]{1,0:T(2,128)(2,1)S(1)} %get-tuple-element.445), channel_id=2, replica_groups=mesh['section'=4,'seq'=2,'tp'=4] {'seq','tp'}, dimensions={1}, use_global_device_ids=true | all-gather | bytes 18432 | tf_op jit(solution)/shard_map/while/body/eval_jaxpr/all_gather | solution.py:84
  148.6 17.0 %all-gather.9.cloned.1.call-done = bf16[64,8192]{1,0:T(8,128)(2,1)} async-done(((bf16[64,1024]{1,0:T(8,128)(2,1)}), bf16[64,8192]{1,0:T(8,128)(2,1)}) %all-gather.9.cloned.1.call-update) | async-done | bytes 1048592 | tf_op jit(solution)/shard_map/while/body/eval_jaxpr/all_gather | solution.py:83
  165.6 1.5 fusion.39
  167.2 4.3 %convolution_add_fusion.3 = f32[64,384]{1,0:T(8,128)S(1)} fusion(bf16[8192,384]{1,0:T(8,128)(2,1)} %get-tuple-element.446, bf16[64,8192]{1,0:T(8,128)(2,1)} %all-gather.9.cloned.1.call-done, f32[8192]{0:T(1024)S(1)} %bitcast.38, f32[64]{0:T(128)S(1)} %add_rsqrt_fusion.2, f32[384]{0:T(512)S(1)} %get-tuple-element.447), kind=kOutput, calls=%fused_computation.8.clone.1 | convolution fusion | flops 404774912 | bytes 7472896 | tf_op jit(solution)/shard_map/while/body/eval_jaxpr/dot_general | solution.py:89
  172.0 9.1 %all_gather.37 = bf16[64,1024]{1,0:T(8,128)(2,1)S(1)} all-gather(bf16[64,128]{1,0:T(8,128)(2,1)S(1)} %convolution_convert_fusion.2), channel_id=1, replica_groups=mesh['section'=4,'seq'=2,'tp'=4] {'seq','tp'}, dimensions={1}, use_global_device_ids=true | all-gather | bytes 147456 | tf_op jit(solution)/shard_map/while/body/eval_jaxpr/all_gather | solution.py:106
  181.7 1.3 collective-permute-start
  183.0 5.5 %collective-permute-done = bf16[64,1024]{1,0:T(8,128)(2,1)S(1)} collective-permute-done((bf16[64,1024]{1,0:T(8,128)(2,1)S(1)}, bf16[64,1024]{1,0:T(8,128)(2,1)S(1)}, u32[]{:S(2)}, u32[]{:S(2)}) %collective-permute-start) | collective-permute-done | bytes 131104 | tf_op jit(solution)/shard_map/while/body/eval_jaxpr/ppermute | solution.py:18
  189.2 8.9 %all-gather.3 = bf16[1,8192]{1,0:T(2,128)(2,1)S(1)} all-gather(bf16[1,1024]{1,0:T(2,128)(2,1)S(1)} %get-tuple-element.445), channel_id=2, replica_groups=mesh['section'=4,'seq'=2,'tp'=4] {'seq','tp'}, dimensions={1}, use_global_device_ids=true | all-gather | bytes 18432 | tf_op jit(solution)/shard_map/while/body/eval_jaxpr/all_gather | solution.py:84
  198.2 17.0 %all-gather.9.cloned.1.call-done = bf16[64,8192]{1,0:T(8,128)(2,1)} async-done(((bf16[64,1024]{1,0:T(8,128)(2,1)}), bf16[64,8192]{1,0:T(8,128)(2,1)}) %all-gather.9.cloned.1.call-update) | async-done | bytes 1048592 | tf_op jit(solution)/shard_map/while/body/eval_jaxpr/all_gather | solution.py:83
  215.2 1.5 fusion.39
  216.7 4.3 %convolution_add_fusion.3 = f32[64,384]{1,0:T(8,128)S(1)} fusion(bf16[8192,384]{1,0:T(8,128)(2,1)} %get-tuple-element.446, bf16[64,8192]{1,0:T(8,128)(2,1)} %all-gather.9.cloned.1.call-done, f32[8192]{0:T(1024)S(1)} %bitcast.38, f32[64]{0:T(128)S(1)} %add_rsqrt_fusion.2, f32[384]{0:T(512)S(1)} %get-tuple-element.447), kind=kOutput, calls=%fused_computation.8.clone.1 | convolution fusion | flops 404774912 | bytes 7472896 | tf_op jit(solution)/shard_map/while/body/eval_jaxpr/dot_general | solution.py:89
  221.6 9.1 %all_gather.37 = bf16[64,1024]{1,0:T(8,128)(2,1)S(1)} all-gather(bf16[64,128]{1,0:T(8,128)(2,1)S(1)} %convolution_convert_fusion.2), channel_id=1, replica_groups=mesh['section'=4,'seq'=2,'tp'=4] {'seq','tp'}, dimensions={1}, use_global_device_ids=true | all-gather | bytes 147456 | tf_op jit(solution)/shard_map/while/body/eval_jaxpr/all_gather | solution.py:106
  231.2 1.3 collective-permute-start
  232.5 5.5 %collective-permute-done = bf16[64,1024]{1,0:T(8,128)(2,1)S(1)} collective-permute-done((bf16[64,1024]{1,0:T(8,128)(2,1)S(1)}, bf16[64,1024]{1,0:T(8,128)(2,1)S(1)}, u32[]{:S(2)}, u32[]{:S(2)}) %collective-permute-start) | collective-permute-done | bytes 131104 | tf_op jit(solution)/shard_map/while/body/eval_jaxpr/ppermute | solution.py:18
  238.8 8.9 %all-gather.3 = bf16[1,8192]{1,0:T(2,128)(2,1)S(1)} all-gather(bf16[1,1024]{1,0:T(2,128)(2,1)S(1)} %get-tuple-element.445), channel_id=2, replica_groups=mesh['section'=4,'seq'=2,'tp'=4] {'seq','tp'}, dimensions={1}, use_global_device_ids=true | all-gather | bytes 18432 | tf_op jit(solution)/shard_map/while/body/eval_jaxpr/all_gather | solution.py:84
  247.8 17.0 %all-gather.9.cloned.1.call-done = bf16[64,8192]{1,0:T(8,128)(2,1)} async-done(((bf16[64,1024]{1,0:T(8,128)(2,1)}), bf16[64,8192]{1,0:T(8,128)(2,1)}) %all-gather.9.cloned.1.call-update) | async-done | bytes 1048592 | tf_op jit(solution)/shard_map/while/body/eval_jaxpr/all_gather | solution.py:83
  264.7 1.5 fusion.39
  266.3 4.3 %convolution_add_fusion.3 = f32[64,384]{1,0:T(8,128)S(1)} fusion(bf16[8192,384]{1,0:T(8,128)(2,1)} %get-tuple-element.446, bf16[64,8192]{1,0:T(8,128)(2,1)} %all-gather.9.cloned.1.call-done, f32[8192]{0:T(1024)S(1)} %bitcast.38, f32[64]{0:T(128)S(1)} %add_rsqrt_fusion.2, f32[384]{0:T(512)S(1)} %get-tuple-element.447), kind=kOutput, calls=%fused_computation.8.clone.1 | convolution fusion | flops 404774912 | bytes 7472896 | tf_op jit(solution)/shard_map/while/body/eval_jaxpr/dot_general | solution.py:89
  271.2 9.1 %all_gather.37 = bf16[64,1024]{1,0:T(8,128)(2,1)S(1)} all-gather(bf16[64,128]{1,0:T(8,128)(2,1)S(1)} %convolution_convert_fusion.2), channel_id=1, replica_groups=mesh['section'=4,'seq'=2,'tp'=4] {'seq','tp'}, dimensions={1}, use_global_device_ids=true | all-gather | bytes 147456 | tf_op jit(solution)/shard_map/while/body/eval_jaxpr/all_gather | solution.py:106
  280.8 1.3 collective-permute-start
  282.1 5.5 %collective-permute-done = bf16[64,1024]{1,0:T(8,128)(2,1)S(1)} collective-permute-done((bf16[64,1024]{1,0:T(8,128)(2,1)S(1)}, bf16[64,1024]{1,0:T(8,128)(2,1)S(1)}, u32[]{:S(2)}, u32[]{:S(2)}) %collective-permute-start) | collective-permute-done | bytes 131104 | tf_op jit(solution)/shard_map/while/body/eval_jaxpr/ppermute | solution.py:18
  287.6 0.7 copy-done.2
  (81 shorter events, 8.5 us)
Async XLA Ops:
  6.5 32.1 %all-gather.7.cloned.1.call-start = ((), (), s32[]{:S(2)}) async-start(), calls=%async_computation | async-start | bytes 2359296 | tf_op jit(solution)/shard_map/all_gather | solution.py:52
  18.4 21.2 %copy-start.3 = (bf16[128,1024]{1,0:T(8,128)(2,1)S(1)}, bf16[128,1024]{1,0:T(8,128)(2,1)}, u32[]{:S(2)}) copy-start(bf16[128,1024]{1,0:T(8,128)(2,1)} %param.11) | copy-start | bytes 786436
  18.4 21.5 %copy-start = (bf16[1,1024,1024]{2,1,0:T(8,128)(2,1)S(1)}, bf16[1,1024,1024]{2,1,0:T(8,128)(2,1)}, u32[]{:S(2)}) copy-start(bf16[1,1024,1024]{2,1,0:T(8,128)(2,1)} %param.19) | copy-start | bytes 6291460
  18.4 21.5 %copy-start.4 = (bf16[1,1024]{1,0:T(2,128)(2,1)S(1)}, bf16[1,1024]{1,0:T(2,128)(2,1)}, u32[]{:S(2)}) copy-start(bf16[1,1024]{1,0:T(2,128)(2,1)} %param.14) | copy-start | bytes 6148
  39.9 26.3 %all-gather.9.cloned.1.call-start = ((), (), s32[]{:S(2)}) async-start(), calls=%async_computation.1 | async-start | bytes 1179648 | tf_op jit(solution)/shard_map/while/body/eval_jaxpr/all_gather | solution.py:83
  67.7 14.0 %copy-start.1 = (bf16[64,1024]{1,0:T(8,128)(2,1)S(1)}, bf16[64,1024]{1,0:T(8,128)(2,1)}, u32[]{:S(2)}) copy-start(bf16[64,1024]{1,0:T(8,128)(2,1)} %bitcast_select_fusion.3) | copy-start | bytes 393220 | tf_op jit(solution)/shard_map/while
  82.2 6.8 %collective-permute-start = (bf16[64,1024]{1,0:T(8,128)(2,1)S(1)}, bf16[64,1024]{1,0:T(8,128)(2,1)S(1)}, u32[]{:S(2)}, u32[]{:S(2)}) collective-permute-start(bf16[64,1024]{1,0:T(8,128)(2,1)S(1)} %get-tuple-element.408), channel_id=1, source_target_pairs={{0,8},{8,16},{16,24},{1,9},{9,17},{17,25},{2,10},{10,18},{18,26},{... | collective-permute-start | bytes 393224 | tf_op jit(solution)/shard_map/while/body/eval_jaxpr/ppermute | solution.py:18
  89.1 27.0 %all-gather.9.cloned.1.call-start = ((), (), s32[]{:S(2)}) async-start(), calls=%async_computation.1 | async-start | bytes 1179648 | tf_op jit(solution)/shard_map/while/body/eval_jaxpr/all_gather | solution.py:83
  117.6 14.0 %copy-start.1 = (bf16[64,1024]{1,0:T(8,128)(2,1)S(1)}, bf16[64,1024]{1,0:T(8,128)(2,1)}, u32[]{:S(2)}) copy-start(bf16[64,1024]{1,0:T(8,128)(2,1)} %bitcast_select_fusion.3) | copy-start | bytes 393220 | tf_op jit(solution)/shard_map/while
  132.1 6.8 %collective-permute-start = (bf16[64,1024]{1,0:T(8,128)(2,1)S(1)}, bf16[64,1024]{1,0:T(8,128)(2,1)S(1)}, u32[]{:S(2)}, u32[]{:S(2)}) collective-permute-start(bf16[64,1024]{1,0:T(8,128)(2,1)S(1)} %get-tuple-element.408), channel_id=1, source_target_pairs={{0,8},{8,16},{16,24},{1,9},{9,17},{17,25},{2,10},{10,18},{18,26},{... | collective-permute-start | bytes 393224 | tf_op jit(solution)/shard_map/while/body/eval_jaxpr/ppermute | solution.py:18
  138.9 26.7 %all-gather.9.cloned.1.call-start = ((), (), s32[]{:S(2)}) async-start(), calls=%async_computation.1 | async-start | bytes 1179648 | tf_op jit(solution)/shard_map/while/body/eval_jaxpr/all_gather | solution.py:83
  167.1 14.0 %copy-start.1 = (bf16[64,1024]{1,0:T(8,128)(2,1)S(1)}, bf16[64,1024]{1,0:T(8,128)(2,1)}, u32[]{:S(2)}) copy-start(bf16[64,1024]{1,0:T(8,128)(2,1)} %bitcast_select_fusion.3) | copy-start | bytes 393220 | tf_op jit(solution)/shard_map/while
  181.7 6.8 %collective-permute-start = (bf16[64,1024]{1,0:T(8,128)(2,1)S(1)}, bf16[64,1024]{1,0:T(8,128)(2,1)S(1)}, u32[]{:S(2)}, u32[]{:S(2)}) collective-permute-start(bf16[64,1024]{1,0:T(8,128)(2,1)S(1)} %get-tuple-element.408), channel_id=1, source_target_pairs={{0,8},{8,16},{16,24},{1,9},{9,17},{17,25},{2,10},{10,18},{18,26},{... | collective-permute-start | bytes 393224 | tf_op jit(solution)/shard_map/while/body/eval_jaxpr/ppermute | solution.py:18
  188.5 26.7 %all-gather.9.cloned.1.call-start = ((), (), s32[]{:S(2)}) async-start(), calls=%async_computation.1 | async-start | bytes 1179648 | tf_op jit(solution)/shard_map/while/body/eval_jaxpr/all_gather | solution.py:83
  216.7 14.0 %copy-start.1 = (bf16[64,1024]{1,0:T(8,128)(2,1)S(1)}, bf16[64,1024]{1,0:T(8,128)(2,1)}, u32[]{:S(2)}) copy-start(bf16[64,1024]{1,0:T(8,128)(2,1)} %bitcast_select_fusion.3) | copy-start | bytes 393220 | tf_op jit(solution)/shard_map/while
  231.2 6.8 %collective-permute-start = (bf16[64,1024]{1,0:T(8,128)(2,1)S(1)}, bf16[64,1024]{1,0:T(8,128)(2,1)S(1)}, u32[]{:S(2)}, u32[]{:S(2)}) collective-permute-start(bf16[64,1024]{1,0:T(8,128)(2,1)S(1)} %get-tuple-element.408), channel_id=1, source_target_pairs={{0,8},{8,16},{16,24},{1,9},{9,17},{17,25},{2,10},{10,18},{18,26},{... | collective-permute-start | bytes 393224 | tf_op jit(solution)/shard_map/while/body/eval_jaxpr/ppermute | solution.py:18
  238.1 26.7 %all-gather.9.cloned.1.call-start = ((), (), s32[]{:S(2)}) async-start(), calls=%async_computation.1 | async-start | bytes 1179648 | tf_op jit(solution)/shard_map/while/body/eval_jaxpr/all_gather | solution.py:83
  266.3 14.0 %copy-start.1 = (bf16[64,1024]{1,0:T(8,128)(2,1)S(1)}, bf16[64,1024]{1,0:T(8,128)(2,1)}, u32[]{:S(2)}) copy-start(bf16[64,1024]{1,0:T(8,128)(2,1)} %bitcast_select_fusion.3) | copy-start | bytes 393220 | tf_op jit(solution)/shard_map/while
  280.8 6.8 %collective-permute-start = (bf16[64,1024]{1,0:T(8,128)(2,1)S(1)}, bf16[64,1024]{1,0:T(8,128)(2,1)S(1)}, u32[]{:S(2)}, u32[]{:S(2)}) collective-permute-start(bf16[64,1024]{1,0:T(8,128)(2,1)S(1)} %get-tuple-element.408), channel_id=1, source_target_pairs={{0,8},{8,16},{16,24},{1,9},{9,17},{17,25},{2,10},{10,18},{18,26},{... | collective-permute-start | bytes 393224 | tf_op jit(solution)/shard_map/while/body/eval_jaxpr/ppermute | solution.py:18
  287.6 0.7 copy-start.2
Sparse Core Ops, SparseCore 0:
  9.2 29.2 all-gather.6
  42.6 23.4 all-gather.8
  91.8 24.1 all-gather.8
  141.4 24.1 all-gather.8
  190.9 24.1 all-gather.8
  240.5 24.1 all-gather.8
where the time goes:
time: 297 us; the launch traced here: 295 us
  waiting for transfers between devices  127 us (43%)
  blocking collectives  96.6 us (33%)
  matrix products  26.6 us (9%)
  other arithmetic  20.1 us (7%)
  between operations  14.1 us (5%)
  starting transfers between devices  6.51 us (2%)
  local copies, waits for them, and re-layouts  4.03 us (1%)
    all_gather x5, waiting for transfers between devices, apply_layer(): lax.all_gather(current, ('seq', 'tp'), axis=1, tiled=True)  84.5 us
    all_gather x5, blocking collectives, apply_layer(): lax.all_gather(context, ('seq', 'tp'), axis=1, tiled=True)  45.5 us
    all_gather x5, blocking collectives, apply_layer(): lax.all_gather(norm_gain[0], ('seq', 'tp'), axis=0, tiled=True)  44.7 us
    ppermute x5, waiting for transfers between devices, from_behind(): return lax.ppermute(block, axis, route)  27.7 us
    dot_general x5, matrix products, apply_layer(): jnp.dot(normed, joint_weight, preferred_element_type=jnp.float32)  21.7 us
    all_gather x1, waiting for transfers between devices, per_device(): lax.all_gather(image_rows, ('seq', 'tp'), axis=0, tiled=True)  13.7 us
    reduce_sum x5, other arithmetic, apply_layer(): jnp.mean(whole_res * whole_res, axis=1, keepdims=True) + EPS  7.64 us
    concatenate x1, other arithmetic, per_device(): jnp.concatenate([q_weight[0], kv_weight[0].reshape(feat_width, 2 * head_s...  6.51 us
  transfers between devices with their start and end apart: 11, of which 11 were waited for; matrix products, arithmetic and copies ran while one was open for 4% of the time, Pallas kernels for 0%

commit v1 on v0

v1 whole, which is shorter than its diff:
```python
import functools
import math

import jax
import jax.numpy as jnp
import numpy as np
from jax import lax
from jax.experimental import pallas as pl
from jax.experimental.pallas import tpu as pltpu
from jax.sharding import PartitionSpec as P

MICRO = 2
EPS = 1e-06
THETA = 1000000.0
LANES = 128
MESH = pl.DeviceIdType.MESH


def tables(tok_count, head_size):
    half_size = head_size // 2
    frequency = np.float32(THETA) ** (
        -np.arange(half_size, dtype=np.float32) * np.float32(2.0) / np.float32(head_size)
    )
    angles = np.arange(tok_count, dtype=np.float32)[:, None] * frequency[None, :]
    cosine = np.concatenate([np.cos(angles), np.cos(angles)], axis=-1)
    signed_sine = np.concatenate([-np.sin(angles), np.sin(angles)], axis=-1)
    return cosine.astype(np.float32), signed_sine.astype(np.float32)


def rotate(values, cosine, signed_sine):
    return values * cosine + pltpu.roll(values, values.shape[1] // 2, 1) * signed_sine


def kernel(
    cfg,
    text,
    img,
    target,
    gain,
    q_hbm,
    q_bias,
    kv_hbm,
    kv_bias,
    out_hbm,
    cos_ref,
    sin_ref,
    out,
    w_all,
    w_out,
    rows,
    ctx,
    images,
    marks,
    gains,
    load_sem,
    z_send,
    z_recv,
    far_send,
    far_recv,
    fwd_send,
    fwd_recv,
    ctx_send,
    ctx_recv,
    gain_send,
    gain_recv,
    img_send,
    img_recv,
    mark_send,
    mark_recv,
):
    sections, seqs, tps, chunks = cfg
    members = seqs * tps
    sec = lax.axis_index("section")
    my_s = lax.axis_index("seq")
    my_t = lax.axis_index("tp")
    me = my_s * tps + my_t
    mate = {"seq": my_s, "tp": my_t + 1 - 2 * lax.rem(my_t, 2)}
    mate_t = mate["tp"]
    toks = text.shape[0] // MICRO
    width = text.shape[1]
    cw = width // chunks
    hd = q_hbm.shape[1]
    slots_own = img.shape[0]
    slots = slots_own * members // MICRO
    is_first = sec == 0

    loads = [
        pltpu.make_async_copy(q_hbm, w_all.at[:, pl.ds(0, hd)], load_sem.at[0]),
        pltpu.make_async_copy(kv_hbm, w_all.at[:, pl.ds(hd, 2 * hd)], load_sem.at[1]),
        pltpu.make_async_copy(out_hbm, w_out, load_sem.at[2]),
    ]
    for load in loads:
        load.start()

    def at_offset(ds, dt, sign=1, base_t=None):
        base = my_t if base_t is None else base_t
        s = lax.rem(my_s + sign * ds + seqs, seqs)
        t = lax.rem(base + sign * dt + tps, tps)
        return s, t

    offsets = [(ds, dt) for ds in range(seqs) for dt in range(tps) if (ds, dt) != (0, 0)]
    far = [(ds, dt) for ds in range(seqs) for dt in range(0, tps, 2) if (ds, dt) != (0, 0)]

    def remote(src, dst, send, recv, device):
        return pltpu.make_async_remote_copy(
            src_ref=src,
            dst_ref=dst,
            send_sem=send,
            recv_sem=recv,
            device_id=device,
            device_id_type=MESH,
        )

    barrier = pltpu.get_barrier_semaphore()
    for ds, dt in offsets:
        s, t = at_offset(ds, dt)
        pl.semaphore_signal(barrier, inc=1, device_id={"seq": s, "tp": t}, device_id_type=MESH)

    @pl.when(sec > 0)
    def _():
        pl.semaphore_signal(barrier, inc=1, device_id={"section": sec - 1}, device_id_type=MESH)

    for j in range(width // LANES):
        gains[me, j : j + 1, :] = gain[0:1, j * LANES : (j + 1) * LANES].astype(jnp.float32)
    lane = lax.broadcasted_iota(jnp.int32, (8, LANES), 1)
    row = lax.broadcasted_iota(jnp.int32, (8, LANES), 0)
    tile = jnp.full((8, LANES), -1, jnp.int32)
    for k in range(slots_own):
        spot = me * slots_own + k
        here = (row == lax.div(spot, slots)) & (lane == lax.rem(spot, slots))
        tile = jnp.where(here, target[k], tile)
    marks[me] = tile
    images[me] = img[:, pl.ds(pl.multiple_of(me * width, width), width)]

    @pl.when(sec == sections - 1)
    def _():
        pl.semaphore_wait(barrier, members - 1)

    @pl.when(sec < sections - 1)
    def _():
        pl.semaphore_wait(barrier, members)

    def img_copy(i):
        s, t = at_offset(*offsets[i])
        peer = s * tps + t
        cols = pl.ds(pl.multiple_of(peer * width, width), width)
        dev = {"seq": s, "tp": t}
        return (
            remote(img.at[:, cols], images.at[me], img_send.at[i], img_recv.at[i], dev),
            remote(marks.at[me], marks.at[me], mark_send.at[i], mark_recv.at[i], dev),
        )

    def gain_copy(i):
        s, t = at_offset(*offsets[i])
        return remote(
            gains.at[me], gains.at[me], gain_send.at[i], gain_recv.at[i], {"seq": s, "tp": t}
        )

    def source(i):
        s, t = at_offset(*offsets[i], sign=-1)
        return s * tps + t

    @pl.when(is_first)
    def _():
        for i in range(len(offsets)):
            for copy in img_copy(i):
                copy.start()

    for i in range(len(offsets)):
        gain_copy(i).start()

    @pl.when(is_first)
    def _():
        for i in range(len(offsets)):
            p = source(i)
            remote(
                marks.at[p], marks.at[p], mark_send.at[i], mark_recv.at[i], mate
            ).wait_recv()
            remote(
                images.at[p], images.at[p], img_send.at[i], img_recv.at[i], mate
            ).wait_recv()
        merged = marks[0]
        for p in range(1, members):
            merged = jnp.maximum(merged, marks[p])
        position = lax.broadcasted_iota(jnp.int32, (toks, slots), 0)
        per_mb = members // MICRO
        for m in range(MICRO):
            match = jnp.where(merged[m : m + 1, :slots] == position, 1.0, 0.0)
            stack = jnp.concatenate(
                [images[m * per_mb + p].astype(jnp.float32) for p in range(per_mb)], axis=0
            ).astype(jnp.bfloat16)
            placed = jnp.dot(
                match.astype(jnp.bfloat16), stack, preferred_element_type=jnp.float32
            )
            is_image = jnp.max(match, axis=1, keepdims=True) > 0.5
            plain = text[m * toks : (m + 1) * toks, :].astype(jnp.float32)
            rows[m, me] = jnp.where(is_image, placed, plain).astype(jnp.bfloat16)

    def cols_of(c):
        return pl.ds(c * cw, cw)

    def z_copy(m, c):
        return remote(
            out.at[0, pl.ds(m * toks, toks), cols_of(c)],
            rows.at[m, me, :, cols_of(c)],
            z_send.at[m, c],
            z_recv.at[m, c],
            {"section": lax.rem(sec + 1, sections)},
        )

    def own_to(m, c, i):
        s, t = at_offset(*far[i])
        ref = rows.at[m, me, :, cols_of(c)]
        return remote(
            ref, ref, far_send.at[m, c, i], far_recv.at[m, c, i], {"seq": s, "tp": t}
        )

    def far_piece(i):
        s, t = at_offset(*far[i], sign=-1)
        return s * tps + t

    def to_mate(m, c, i):
        piece = me if i == 0 else far_piece(i - 1)
        ref = rows.at[m, piece, :, cols_of(c)]
        return remote(ref, ref, fwd_send.at[m, c, i], fwd_recv.at[m, c, i], mate)

    def mate_piece(i):
        ds, dt = (0, 0) if i == 0 else far[i - 1]
        s, t = at_offset(ds, dt, sign=-1, base_t=mate_t)
        return s * tps + t

    def launch(m):
        for c in range(chunks):

            @pl.when(sec > 0)
            def _():
                z_copy(m, c).wait_recv()

            for i in range(len(far)):
                own_to(m, c, i).start()
            to_mate(m, c, 0).start()

    def piece_step(m, p, c, carry):
        total, squares = carry
        piece = rows[m, p, :, c * cw : (c + 1) * cw].astype(jnp.float32)
        first = c * cw // LANES
        scale = jnp.concatenate(
            [gains[p, pl.ds(first + j, 1), :] for j in range(cw // LANES)], axis=1
        )
        for j in range(cw // LANES):
            part = piece[:, j * LANES : (j + 1) * LANES]
            squares = squares + part * part
        weight = w_all[pl.ds(pl.multiple_of(p * width + c * cw, cw), cw), :]
        total = total + jnp.dot(
            (piece * scale).astype(jnp.bfloat16), weight, preferred_element_type=jnp.float32
        )
        return total, squares

    def project(m):
        carry = (
            jnp.zeros((toks, 3 * hd), jnp.float32),
            jnp.zeros((toks, LANES), jnp.float32),
        )
        for c in range(chunks):
            carry = piece_step(m, me, c, carry)
        for c in range(chunks):
            p = mate_piece(0)
            ref = rows.at[m, p, :, cols_of(c)]
            remote(ref, ref, fwd_send.at[m, c, 0], fwd_recv.at[m, c, 0], mate).wait_recv()
            carry = piece_step(m, p, c, carry)
        for c in range(chunks):
            for i in range(len(far)):
                p = far_piece(i)
                ref = rows.at[m, p, :, cols_of(c)]
                remote(
                    ref, ref, far_send.at[m, c, i], far_recv.at[m, c, i], mate
                ).wait_recv()
                to_mate(m, c, i + 1).start()
                carry = piece_step(m, p, c, carry)
            for i in range(len(far)):
                p = mate_piece(i + 1)
                ref = rows.at[m, p, :, cols_of(c)]
                remote(
                    ref, ref, fwd_send.at[m, c, i + 1], fwd_recv.at[m, c, i + 1], mate
                ).wait_recv()
                carry = piece_step(m, p, c, carry)
        return carry

    def ctx_copy(m, i):
        s, t = at_offset(*offsets[i])
        ref = ctx.at[m, :, pl.ds(pl.multiple_of(me * hd, hd), hd)]
        return remote(ref, ref, ctx_send.at[m, i], ctx_recv.at[m, i], {"seq": s, "tp": t})

    bias = jnp.concatenate([q_bias[...], kv_bias[...]], axis=1).astype(jnp.float32)
    cosine = cos_ref[...]
    signed_sine = sin_ref[...]
    query_at = lax.broadcasted_iota(jnp.int32, (toks, toks), 0)
    key_at = lax.broadcasted_iota(jnp.int32, (toks, toks), 1)

    def attend(m, carry):
        total, squares = carry
        mean = jnp.sum(squares, axis=1, keepdims=True) / (width * members)
        biased = total * lax.rsqrt(mean + EPS) + bias
        queries = rotate(biased[:, :hd], cosine, signed_sine).astype(jnp.bfloat16)
        keys = rotate(biased[:, hd : 2 * hd], cosine, signed_sine).astype(jnp.bfloat16)
        values = biased[:, 2 * hd :].astype(jnp.bfloat16)
        scores = lax.dot_general(
            queries, keys, (((1,), (1,)), ((), ())), preferred_element_type=jnp.float32
        )
        scores = jnp.where(query_at >= key_at, scores * (1.0 / math.sqrt(hd)), -1e30)
        expo = jnp.exp(scores - jnp.max(scores, axis=1, keepdims=True))
        probs = (expo / jnp.sum(expo, axis=1, keepdims=True)).astype(jnp.bfloat16)
        context = jnp.dot(probs, values, preferred_element_type=jnp.float32)
        ctx[m, :, pl.ds(pl.multiple_of(me * hd, hd), hd)] = context.astype(jnp.bfloat16)
        for i in range(len(offsets)):
            ctx_copy(m, i).start()

    def finish(m):
        for i in range(len(offsets)):
            p = source(i)
            ref = ctx.at[m, :, pl.ds(pl.multiple_of(p * hd, hd), hd)]
            remote(ref, ref, ctx_send.at[m, i], ctx_recv.at[m, i], mate).wait_recv()
        for c in range(chunks):
            update = jnp.dot(
                ctx[m], w_out[:, c * cw : (c + 1) * cw], preferred_element_type=jnp.float32
            )
            before = rows[m, me, :, c * cw : (c + 1) * cw].astype(jnp.float32)
            out[0, m * toks : (m + 1) * toks, c * cw : (c + 1) * cw] = (before + update).astype(
                jnp.bfloat16
            )

            @pl.when(sec < sections - 1)
            def _():
                z_copy(m, c).start()

    launch(0)
    for i in range(len(offsets)):
        p = source(i)
        remote(
            gains.at[p], gains.at[p], gain_send.at[i], gain_recv.at[i], mate
        ).wait_recv()
    loads[0].wait()
    loads[1].wait()
    attend(0, project(0))
    loads[2].wait()
    for m in range(MICRO):
        if m + 1 < MICRO:
            launch(m + 1)
        finish(m)
        if m + 1 < MICRO:
            attend(m + 1, project(m + 1))

    for m in range(MICRO):
        for c in range(chunks):
            for i in range(len(far)):
                own_to(m, c, i).wait_send()
            for i in range(len(far) + 1):
                to_mate(m, c, i).wait_send()

            @pl.when(sec < sections - 1)
            def _():
                z_copy(m, c).wait_send()

        for i in range(len(offsets)):
            ctx_copy(m, i).wait_send()
    for i in range(len(offsets)):
        gain_copy(i).wait_send()

    @pl.when(is_first)
    def _():
        for i in range(len(offsets)):
            for copy in img_copy(i):
                copy.wait_send()


def per_device(
    sizes,
    text_rows,
    image_rows,
    image_target,
    norm_gain,
    q_weight,
    q_bias,
    kv_weight,
    kv_bias,
    out_weight,
):
    sections, seqs, tps = sizes
    members = seqs * tps
    tok_count = text_rows.shape[0] // MICRO
    width = text_rows.shape[1]
    head_size = q_weight.shape[2]
    chunks = 2 if width >= 512 else 1
    features = width * members
    cosine, signed_sine = tables(tok_count, head_size)
    others = members - 1
    far = seqs * tps // 2 - 1
    vmem = pl.BlockSpec(memory_space=pltpu.VMEM)
    hbm = pl.BlockSpec(memory_space=pl.ANY)
    smem = pl.BlockSpec(memory_space=pltpu.SMEM)
    dma = pltpu.SemaphoreType.DMA
    bf16 = jnp.bfloat16
    return pl.pallas_call(
        functools.partial(kernel, (sections, seqs, tps, chunks)),
        out_shape=jax.ShapeDtypeStruct((1, MICRO * tok_count, width), bf16),
        in_specs=[vmem, vmem, smem, vmem, hbm, vmem, hbm, vmem, hbm, vmem, vmem],
        out_specs=vmem,
        scratch_shapes=[
            pltpu.VMEM((features, 3 * head_size), bf16),
            pltpu.VMEM((members * head_size, width), bf16),
            pltpu.VMEM((MICRO, members, tok_count, width), bf16),
            pltpu.VMEM((MICRO, tok_count, members * head_size), bf16),
            pltpu.VMEM((members, image_rows.shape[0], width), bf16),
            pltpu.VMEM((members, 8, LANES), jnp.int32),
            pltpu.VMEM((members, 8, LANES), jnp.float32),
            dma((3,)),
            dma((MICRO, chunks)),
            dma((MICRO, chunks)),
            dma((MICRO, chunks, far)),
            dma((MICRO, chunks, far)),
            dma((MICRO, chunks, far + 1)),
            dma((MICRO, chunks, far + 1)),
            dma((MICRO, others)),
            dma((MICRO, others)),
            dma((others,)),
            dma((others,)),
            dma((others,)),
            dma((others,)),
            dma((others,)),
            dma((others,)),
        ],
        compiler_params=pltpu.CompilerParams(
            collective_id=0, has_side_effects=True, vmem_limit_bytes=40 * 1024 * 1024
        ),
    )(
        text_rows,
        image_rows,
        image_target,
        norm_gain,
        q_weight[0],
        q_bias,
        kv_weight[0].reshape(features, 2 * head_size),
        kv_bias[0],
        out_weight[0],
        jnp.asarray(cosine),
        jnp.asarray(signed_sine),
    )


def solution(mesh):
    sizes = tuple(mesh.shape[axis] for axis in ("section", "seq", "tp"))
    in_specs = (
        P(None, ("seq", "tp")),
        P(("seq", "tp"), None),
        P(("seq", "tp")),
        P("section", ("seq", "tp")),
        P("section", None, ("seq", "tp")),
        P("section", ("seq", "tp")),
        P("section", None, "tp", None),
        P("section", "tp", None),
        P("section", None, ("seq", "tp")),
    )
    out_specs = P("section", None, ("seq", "tp"))
    return jax.shard_map(
        functools.partial(per_device, sizes),
        mesh=mesh,
        in_specs=in_specs,
        out_specs=out_specs,
        check_vma=False,
    )
```

time: 297 us -> 98.4 us (0.33)
  waiting for transfers between devices: 127 us -> 0 us
  blocking collectives: 96.6 us -> 0 us
  Pallas kernels: 0 us -> 85.7 us
  matrix products: 26.6 us -> 0 us
  other arithmetic: 20.1 us -> 0 us
  between operations: 14.1 us -> 0.02 us
  local copies, waits for them, and re-layouts: 4.03 us -> 12.2 us
  starting transfers between devices: 6.51 us -> 0 us
    all_gather x6 -> x0, waiting for transfers between devices: 98.2 us -> none  [the longest x5 84.5 us: apply_layer(): lax.all_gather(current, ('seq', 'tp'), axis=1, tiled=True)]
    all_gather x10 -> x0, blocking collectives: 90.2 us -> none  [the longest x5 45.5 us: apply_layer(): lax.all_gather(context, ('seq', 'tp'), axis=1, tiled=True)]
    pallas_call x0 -> x1, Pallas kernels: none -> 85.7 us  [per_device(): pl.pallas_call(functools.partial(kernel, (sections, seqs, tps, chunks)),...]
    ppermute x5 -> x0, waiting for transfers between devices: 27.7 us -> none  [from_behind(): return lax.ppermute(block, axis, route)]
    dot_general x21 -> x0, matrix products: 26.6 us -> none  [the longest x5 21.7 us: apply_layer(): jnp.dot(normed, joint_weight, preferred_element_type=jnp.float32)]
    unnamed x11 -> x23, local copies, waits for them, and re-layouts: 2.82 us -> 12.2 us
    reduce_sum x10 -> x0, other arithmetic: 7.83 us -> none  [the longest x5 7.64 us: apply_layer(): jnp.mean(whole_res * whole_res, axis=1, keepdims=True) + EPS]
    concatenate x2 -> x0, other arithmetic: 6.6 us -> none  [the longest x1 6.51 us: per_device(): jnp.concatenate([q_weight[0], kv_weight[0].reshape(feat_width, 2 * head_s...]
  transfers between devices with their start and end apart: 11 -> 0, of which waited for: 11 -> 0; matrix products, arithmetic and copies ran while one was open for 4% -> 0% of each run, Pallas kernels for 0% -> 0%
where the time goes in v1:
time: 98.4 us; the launch traced here: 97.9 us
  Pallas kernels  85.7 us (87%)
  local copies, waits for them, and re-layouts  12.2 us (12%)
    pallas_call x1, Pallas kernels, per_device(): pl.pallas_call(functools.partial(kernel, (sections, seqs, tps, chunks)),...  85.7 us
    unnamed x23, local copies, waits for them, and re-layouts  12.2 us

profile of v1, /device:TPU:25, one launch (start us, length us, event | category | flops | bytes accessed | tf_op | source)
XLA Modules:
  0.0 97.9 jit_solution(7540307775192204812)
XLA Ops:
  0.0 0.0 copy-start
  0.0 2.2 %copy-done = bf16[1,8192,1,256]{3,1,2,0:T(8,128)(2,1)S(1)} copy-done((bf16[1,8192,1,256]{3,1,2,0:T(8,128)(2,1)S(1)}, bf16[1,8192,1,256]{3,1,2,0:T(8,128)(2,1)}, u32[]{:S(2)}) %copy-start) | copy-done | bytes 4194328
  2.2 0.0 copy-start.1
  2.2 1.6 %copy-done.1 = bf16[1,8192,128]{2,1,0:T(8,128)(2,1)S(1)} copy-done((bf16[1,8192,128]{2,1,0:T(8,128)(2,1)S(1)}, bf16[1,8192,128]{2,1,0:T(8,128)(2,1)}, u32[]{:S(2)}) %copy-start.1) | copy-done | bytes 2097176
  3.8 0.0 copy-start.2
  3.8 1.6 %copy-done.2 = bf16[1,1024,1024]{2,1,0:T(8,128)(2,1)S(1)} copy-done((bf16[1,1024,1024]{2,1,0:T(8,128)(2,1)S(1)}, bf16[1,1024,1024]{2,1,0:T(8,128)(2,1)}, u32[]{:S(2)}) %copy-start.2) | copy-done | bytes 2097176
  5.4 0.0 copy-start.3
  5.4 0.9 copy-done.3
  6.3 0.0 copy-start.4
  6.3 0.9 copy-done.4
  7.3 0.0 copy-start.5
  7.3 0.8 copy-done.5
  8.0 0.0 copy-start.6
  8.0 0.8 copy-done.6
  8.8 0.0 copy-start.7
  8.8 0.7 copy-done.7
  9.5 0.0 copy-start.8
  9.5 0.7 copy-done.8
  10.2 0.0 copy-start.9
  10.2 0.7 copy-done.9
  10.8 0.0 copy-start.10
  10.8 0.7 copy-done.10
  11.5 85.7 %shard_map.109 = bf16[1,128,1024]{2,1,0:T(8,128)(2,1)S(1)} custom-call(bf16[128,1024]{1,0:T(8,128)(2,1)S(1)} %copy-done.3, bf16[16,8192]{1,0:T(8,128)(2,1)S(1)} %copy-done.4, s32[16]{0:T(128)S(1)} %copy-done.9, bf16[1,1024]{1,0:T(2,128)(2,1)S(1)} %copy-done.7, bf16[8192,128]{1,0:T(8,128)(2,1)S(1)} %bitcast.5, bf16[1,128]{1,0:T(2,128)(2,1)S(1)} %copy-done.10, ...), custom_call_target="tpu_custom_call" | custom-call | tf_op jit(solution)/shard_map/pallas_call | solution.py:403
  97.2 0.7 copy.13
Async XLA Ops:
  0.0 2.2 %copy-start = (bf16[1,8192,1,256]{3,1,2,0:T(8,128)(2,1)S(1)}, bf16[1,8192,1,256]{3,1,2,0:T(8,128)(2,1)}, u32[]{:S(2)}) copy-start(bf16[1,8192,1,256]{3,1,2,0:T(8,128)(2,1)} %param.17) | copy-start | bytes 12582916
  2.2 1.6 %copy-start.1 = (bf16[1,8192,128]{2,1,0:T(8,128)(2,1)S(1)}, bf16[1,8192,128]{2,1,0:T(8,128)(2,1)}, u32[]{:S(2)}) copy-start(bf16[1,8192,128]{2,1,0:T(8,128)(2,1)} %param.15) | copy-start | bytes 6291460
  3.8 1.6 %copy-start.2 = (bf16[1,1024,1024]{2,1,0:T(8,128)(2,1)S(1)}, bf16[1,1024,1024]{2,1,0:T(8,128)(2,1)}, u32[]{:S(2)}) copy-start(bf16[1,1024,1024]{2,1,0:T(8,128)(2,1)} %param.19) | copy-start | bytes 6291460
  5.4 0.9 copy-start.3
  6.3 0.9 copy-start.4
  7.3 0.8 copy-start.5
  8.0 0.8 copy-start.6
  8.8 0.7 copy-start.7
  9.5 0.7 copy-start.8
  10.2 0.7 copy-start.9
  10.8 0.7 copy-start.10

commit v2 on v1

--- a/solution.py
+++ b/solution.py
@@ -33,18 +33,23 @@
 
 def kernel(
     cfg,
+    text_hbm,
+    img,
+    target_hbm,
+    gain_hbm,
+    q_hbm,
+    q_bias_hbm,
+    kv_hbm,
+    kv_bias_hbm,
+    out_hbm,
+    table_hbm,
+    out,
     text,
-    img,
     target,
     gain,
-    q_hbm,
     q_bias,
-    kv_hbm,
     kv_bias,
-    out_hbm,
-    cos_ref,
-    sin_ref,
-    out,
+    table,
     w_all,
     w_out,
     rows,
@@ -76,21 +81,13 @@
     me = my_s * tps + my_t
     mate = {"seq": my_s, "tp": my_t + 1 - 2 * lax.rem(my_t, 2)}
     mate_t = mate["tp"]
-    toks = text.shape[0] // MICRO
-    width = text.shape[1]
+    toks = text_hbm.shape[0] // MICRO
+    width = text_hbm.shape[1]
     cw = width // chunks
     hd = q_hbm.shape[1]
     slots_own = img.shape[0]
     slots = slots_own * members // MICRO
     is_first = sec == 0
-
-    loads = [
-        pltpu.make_async_copy(q_hbm, w_all.at[:, pl.ds(0, hd)], load_sem.at[0]),
-        pltpu.make_async_copy(kv_hbm, w_all.at[:, pl.ds(hd, 2 * hd)], load_sem.at[1]),
-        pltpu.make_async_copy(out_hbm, w_out, load_sem.at[2]),
-    ]
-    for load in loads:
-        load.start()
 
     def at_offset(ds, dt, sign=1, base_t=None):
         base = my_t if base_t is None else base_t
@@ -119,6 +116,26 @@
     @pl.when(sec > 0)
     def _():
         pl.semaphore_signal(barrier, inc=1, device_id={"section": sec - 1}, device_id_type=MESH)
+
+    own_cols = pl.ds(pl.multiple_of(me * width, width), width)
+    early = [
+        pltpu.make_async_copy(target_hbm, target, load_sem.at[0]),
+        pltpu.make_async_copy(gain_hbm, gain, load_sem.at[1]),
+        pltpu.make_async_copy(img.at[:, own_cols], images.at[me], load_sem.at[2]),
+        pltpu.make_async_copy(text_hbm, text, load_sem.at[3]),
+    ]
+    loads = [
+        pltpu.make_async_copy(q_hbm, w_all.at[:, pl.ds(0, hd)], load_sem.at[4]),
+        pltpu.make_async_copy(kv_hbm, w_all.at[:, pl.ds(hd, 2 * hd)], load_sem.at[5]),
+        pltpu.make_async_copy(q_bias_hbm, q_bias, load_sem.at[6]),
+        pltpu.make_async_copy(kv_bias_hbm, kv_bias, load_sem.at[7]),
+        pltpu.make_async_copy(table_hbm, table, load_sem.at[8]),
+        pltpu.make_async_copy(out_hbm, w_out, load_sem.at[9]),
+    ]
+    for load in early + loads:
+        load.start()
+    for load in early:
+        load.wait()
 
     for j in range(width // LANES):
         gains[me, j : j + 1, :] = gain[0:1, j * LANES : (j + 1) * LANES].astype(jnp.float32)
@@ -130,7 +147,6 @@
         here = (row == lax.div(spot, slots)) & (lane == lax.rem(spot, slots))
         tile = jnp.where(here, target[k], tile)
     marks[me] = tile
-    images[me] = img[:, pl.ds(pl.multiple_of(me * width, width), width)]
 
     @pl.when(sec == sections - 1)
     def _():
@@ -146,8 +162,8 @@
         cols = pl.ds(pl.multiple_of(peer * width, width), width)
         dev = {"seq": s, "tp": t}
         return (
-            remote(img.at[:, cols], images.at[me], img_send.at[i], img_recv.at[i], dev),
             remote(marks.at[me], marks.at[me], mark_send.at[i], mark_recv.at[i], dev),
+            remote(img.at[:, cols], images.at[me], img_send.at[i], img_recv.at[me], dev),
         )
 
     def gain_copy(i):
@@ -168,6 +184,30 @@
 
     for i in range(len(offsets)):
         gain_copy(i).start()
+
+    per_mb = members // MICRO
+    position = lax.broadcasted_iota(jnp.int32, (toks, slots), 0)
+
+    def embed(m):
+        merged = marks[0]
+        for p in range(1, members):
+            merged = jnp.maximum(merged, marks[p])
+        match = jnp.where(merged[m : m + 1, :slots] == position, 1.0, 0.0)
+        for p in range(m * per_mb, (m + 1) * per_mb):
+
+            @pl.when(me != p)
+            def _():
+                remote(
+                    images.at[p], images.at[p], img_send.at[0], img_recv.at[p], mate
+                ).wait_recv()
+
+        stack = jnp.concatenate(
+            [images[m * per_mb + p].astype(jnp.float32) for p in range(per_mb)], axis=0
+        ).astype(jnp.bfloat16)
+        placed = jnp.dot(match.astype(jnp.bfloat16), stack, preferred_element_type=jnp.float32)
+        is_image = jnp.max(match, axis=1, keepdims=True) > 0.5
+        plain = text[m * toks : (m + 1) * toks, :].astype(jnp.float32)
+        rows[m, me] = jnp.where(is_image, placed, plain).astype(jnp.bfloat16)
 
     @pl.when(is_first)
     def _():
@@ -176,25 +216,7 @@
             remote(
                 marks.at[p], marks.at[p], mark_send.at[i], mark_recv.at[i], mate
             ).wait_recv()
-            remote(
-                images.at[p], images.at[p], img_send.at[i], img_recv.at[i], mate
-            ).wait_recv()
-        merged = marks[0]
-        for p in range(1, members):
-            merged = jnp.maximum(merged, marks[p])
-        position = lax.broadcasted_iota(jnp.int32, (toks, slots), 0)
-        per_mb = members // MICRO
-        for m in range(MICRO):
-            match = jnp.where(merged[m : m + 1, :slots] == position, 1.0, 0.0)
-            stack = jnp.concatenate(
-                [images[m * per_mb + p].astype(jnp.float32) for p in range(per_mb)], axis=0
-            ).astype(jnp.bfloat16)
-            placed = jnp.dot(
-                match.astype(jnp.bfloat16), stack, preferred_element_type=jnp.float32
-            )
-            is_image = jnp.max(match, axis=1, keepdims=True) > 0.5
-            plain = text[m * toks : (m + 1) * toks, :].astype(jnp.float32)
-            rows[m, me] = jnp.where(is_image, placed, plain).astype(jnp.bfloat16)
+        embed(0)
 
     def cols_of(c):
         return pl.ds(c * cw, cw)
@@ -208,6 +230,26 @@
             {"section": lax.rem(sec + 1, sections)},
         )
 
+    relayed = seqs == 2 and tps == 4 and chunks == 2
+    across = far.index((0, 2)) if relayed else None
+    along = far.index((1, 0)) if relayed else None
+    corner = far.index((1, 2)) if relayed else None
+
+    def direct(i):
+        return not relayed or i != corner
+
+    def relay(m, c):
+        got, to = (across, along) if c == 0 else (along, across)
+        s, t = at_offset(*far[to])
+        ref = rows.at[m, far_piece(got), :, cols_of(c)]
+        return remote(
+            ref,
+            ref,
+            far_send.at[m, c, corner],
+            far_recv.at[m, c, corner],
+            {"seq": s, "tp": t},
+        )
+
     def own_to(m, c, i):
         s, t = at_offset(*far[i])
         ref = rows.at[m, me, :, cols_of(c)]
@@ -237,7 +279,8 @@
                 z_copy(m, c).wait_recv()
 
             for i in range(len(far)):
-                own_to(m, c, i).start()
+                if direct(i):
+                    own_to(m, c, i).start()
             to_mate(m, c, 0).start()
 
     def piece_step(m, p, c, carry):
@@ -256,7 +299,22 @@
         )
         return total, squares
 
-    def project(m):
+    def take_far(m, c, i, carry):
+        p = far_piece(i)
+        ref = rows.at[m, p, :, cols_of(c)]
+        remote(ref, ref, far_send.at[m, c, i], far_recv.at[m, c, i], mate).wait_recv()
+        if relayed and i == (across if c == 0 else along):
+            relay(m, c).start()
+        to_mate(m, c, i + 1).start()
+        return piece_step(m, p, c, carry)
+
+    def take_mate(m, c, i, carry):
+        p = mate_piece(i)
+        ref = rows.at[m, p, :, cols_of(c)]
+        remote(ref, ref, fwd_send.at[m, c, i], fwd_recv.at[m, c, i], mate).wait_recv()
+        return piece_step(m, p, c, carry)
+
+    def project_near(m):
         carry = (
             jnp.zeros((toks, 3 * hd), jnp.float32),
             jnp.zeros((toks, LANES), jnp.float32),
@@ -264,26 +322,24 @@
         for c in range(chunks):
             carry = piece_step(m, me, c, carry)
         for c in range(chunks):
-            p = mate_piece(0)
-            ref = rows.at[m, p, :, cols_of(c)]
-            remote(ref, ref, fwd_send.at[m, c, 0], fwd_recv.at[m, c, 0], mate).wait_recv()
-            carry = piece_step(m, p, c, carry)
+            carry = take_mate(m, c, 0, carry)
+        return carry
+
+    def project_far(m, carry):
+        late = [i for i in range(len(far)) if not direct(i)]
+        soon = [i for i in range(len(far)) if direct(i)]
+        for group in (soon, late):
+            for c in range(chunks):
+                order = group if c == 0 else group[::-1]
+                for i in order:
+                    carry = take_far(m, c, i, carry)
+                if group is late:
+                    continue
+                for i in order:
+                    carry = take_mate(m, c, i + 1, carry)
         for c in range(chunks):
-            for i in range(len(far)):
-                p = far_piece(i)
-                ref = rows.at[m, p, :, cols_of(c)]
-                remote(
-                    ref, ref, far_send.at[m, c, i], far_recv.at[m, c, i], mate
-                ).wait_recv()
-                to_mate(m, c, i + 1).start()
-                carry = piece_step(m, p, c, carry)
-            for i in range(len(far)):
-                p = mate_piece(i + 1)
-                ref = rows.at[m, p, :, cols_of(c)]
-                remote(
-                    ref, ref, fwd_send.at[m, c, i + 1], fwd_recv.at[m, c, i + 1], mate
-                ).wait_recv()
-                carry = piece_step(m, p, c, carry)
+            for i in late:
+                carry = take_mate(m, c, i + 1, carry)
         return carry
 
     def ctx_copy(m, i):
@@ -291,14 +347,14 @@
         ref = ctx.at[m, :, pl.ds(pl.multiple_of(me * hd, hd), hd)]
         return remote(ref, ref, ctx_send.at[m, i], ctx_recv.at[m, i], {"seq": s, "tp": t})
 
-    bias = jnp.concatenate([q_bias[...], kv_bias[...]], axis=1).astype(jnp.float32)
-    cosine = cos_ref[...]
-    signed_sine = sin_ref[...]
     query_at = lax.broadcasted_iota(jnp.int32, (toks, toks), 0)
     key_at = lax.broadcasted_iota(jnp.int32, (toks, toks), 1)
 
     def attend(m, carry):
         total, squares = carry
+        bias = jnp.concatenate([q_bias[...], kv_bias[...]], axis=1).astype(jnp.float32)
+        cosine = table[0]
+        signed_sine = table[1]
         mean = jnp.sum(squares, axis=1, keepdims=True) / (width * members)
         biased = total * lax.rsqrt(mean + EPS) + bias
         queries = rotate(biased[:, :hd], cosine, signed_sine).astype(jnp.bfloat16)
@@ -341,19 +397,41 @@
         ).wait_recv()
     loads[0].wait()
     loads[1].wait()
-    attend(0, project(0))
-    loads[2].wait()
+
+    @pl.when(is_first)
+    def _():
+        for m in range(1, MICRO):
+            embed(m)
+
+    carry = project_far(0, project_near(0))
+    for load in loads[2:]:
+        load.wait()
     for m in range(MICRO):
         if m + 1 < MICRO:
-            launch(m + 1)
+
+            @pl.when(is_first)
+            def _():
+                launch(m + 1)
+
+        attend(m, carry)
+        if m + 1 < MICRO:
+
+            @pl.when(sec > 0)
+            def _():
+                launch(m + 1)
+
+            carry = project_near(m + 1)
         finish(m)
         if m + 1 < MICRO:
-            attend(m + 1, project(m + 1))
+            carry = project_far(m + 1, carry)
 
     for m in range(MICRO):
         for c in range(chunks):
             for i in range(len(far)):
-                own_to(m, c, i).wait_send()
+                if direct(i):
+                    own_to(m, c, i).wait_send()
+            if relayed:
+                relay(m, c).wait_send()
             for i in range(len(far) + 1):
                 to_mate(m, c, i).wait_send()
 
@@ -396,16 +474,21 @@
     others = members - 1
     far = seqs * tps // 2 - 1
     vmem = pl.BlockSpec(memory_space=pltpu.VMEM)
-    hbm = pl.BlockSpec(memory_space=pl.ANY)
-    smem = pl.BlockSpec(memory_space=pltpu.SMEM)
+    hbm = pl.BlockSpec(memory_space=pltpu.HBM)
     dma = pltpu.SemaphoreType.DMA
     bf16 = jnp.bfloat16
     return pl.pallas_call(
         functools.partial(kernel, (sections, seqs, tps, chunks)),
         out_shape=jax.ShapeDtypeStruct((1, MICRO * tok_count, width), bf16),
-        in_specs=[vmem, vmem, smem, vmem, hbm, vmem, hbm, vmem, hbm, vmem, vmem],
+        in_specs=[hbm] * 10,
         out_specs=vmem,
         scratch_shapes=[
+            pltpu.VMEM(text_rows.shape, bf16),
+            pltpu.SMEM(image_target.shape, jnp.int32),
+            pltpu.VMEM(norm_gain.shape, bf16),
+            pltpu.VMEM(q_bias.shape, bf16),
+            pltpu.VMEM(kv_bias.shape[1:], bf16),
+            pltpu.VMEM((2, tok_count, head_size), jnp.float32),
             pltpu.VMEM((features, 3 * head_size), bf16),
             pltpu.VMEM((members * head_size, width), bf16),
             pltpu.VMEM((MICRO, members, tok_count, width), bf16),
@@ -413,7 +496,7 @@
             pltpu.VMEM((members, image_rows.shape[0], width), bf16),
             pltpu.VMEM((members, 8, LANES), jnp.int32),
             pltpu.VMEM((members, 8, LANES), jnp.float32),
-            dma((3,)),
+            dma((10,)),
             dma((MICRO, chunks)),
             dma((MICRO, chunks)),
             dma((MICRO, chunks, far)),
@@ -425,12 +508,12 @@
             dma((others,)),
             dma((others,)),
             dma((others,)),
-            dma((others,)),
+            dma((members,)),
             dma((others,)),
             dma((others,)),
         ],
         compiler_params=pltpu.CompilerParams(
-            collective_id=0, has_side_effects=True, vmem_limit_bytes=40 * 1024 * 1024
+            collective_id=0, has_side_effects=True, vmem_limit_bytes=60 * 1024 * 1024
         ),
     )(
         text_rows,
@@ -442,8 +525,7 @@
         kv_weight[0].reshape(features, 2 * head_size),
         kv_bias[0],
         out_weight[0],
-        jnp.asarray(cosine),
-        jnp.asarray(signed_sine),
+        jnp.asarray(np.stack([cosine, signed_sine])),
     )
 
 

time: 98.4 us -> 94.6 us (0.961)
  local copies, waits for them, and re-layouts: 12.2 us -> 1.67 us
  Pallas kernels: 85.7 us -> 92.8 us
    unnamed x23 -> x1, local copies, waits for them, and re-layouts: 12.2 us -> 1.67 us
    pallas_call x1, Pallas kernels: 85.7 us -> 92.8 us  [per_device(): pl.pallas_call(functools.partial(kernel, (sections, seqs, tps, chunks)),...]
where the time goes in v2:
time: 94.6 us; the launch traced here: 94.5 us
  Pallas kernels  92.8 us (98%)
  local copies, waits for them, and re-layouts  1.67 us (2%)
    pallas_call x1, Pallas kernels, per_device(): pl.pallas_call(functools.partial(kernel, (sections, seqs, tps, chunks)),...  92.8 us

profile of v2, /device:TPU:25, one launch (start us, length us, event | category | flops | bytes accessed | tf_op | source)
XLA Modules:
  0.0 94.5 jit_solution(17536152605407181346)
XLA Ops:
  0.0 92.8 %shard_map.100 = bf16[1,128,1024]{2,1,0:T(8,128)(2,1)} custom-call(bf16[128,1024]{1,0:T(8,128)(2,1)} %text_hbm.1, bf16[16,8192]{1,0:T(8,128)(2,1)} %img.1, s32[16]{0:T(128)} %target_hbm.1, bf16[1,1024]{1,0:T(2,128)(2,1)} %gain_hbm.1, bf16[8192,128]{1,0:T(8,128)(2,1)} %bitcast.5, bf16[1,128]{1,0:T(2,128)(2,1)} %q_bias_hbm.1, bf16[8192,256]{1,0:T(8,128)(2,1)} %bitcast.4, ...), custom_call_target="tpu_custom_call" | custom-call | tf_op jit(solution)/shard_map/pallas_call | solution.py:480
  92.8 1.7 %copy.12 = bf16[1,128,1024]{2,1,0:T(8,128)(2,1)} copy(bf16[1,128,1024]{2,1,0:T(8,128)(2,1)} %shard_map.100) | data formatting | bytes 524288

commit v3 on v2

--- a/solution.py
+++ b/solution.py
@@ -414,16 +414,14 @@
                 launch(m + 1)
 
         attend(m, carry)
+        finish(m)
         if m + 1 < MICRO:
 
             @pl.when(sec > 0)
             def _():
                 launch(m + 1)
 
-            carry = project_near(m + 1)
-        finish(m)
-        if m + 1 < MICRO:
-            carry = project_far(m + 1, carry)
+            carry = project_far(m + 1, project_near(m + 1))
 
     for m in range(MICRO):
         for c in range(chunks):

time: 94.6 us -> 98 us (1.036)
  Pallas kernels: 92.8 us -> 96.2 us
    pallas_call x1, Pallas kernels: 92.8 us -> 96.2 us  [per_device(): pl.pallas_call(functools.partial(kernel, (sections, seqs, tps, chunks)),...]
where the time goes in v3:
time: 98 us; the launch traced here: 97.9 us
  Pallas kernels  96.2 us (98%)
  local copies, waits for them, and re-layouts  1.67 us (2%)
    pallas_call x1, Pallas kernels, per_device(): pl.pallas_call(functools.partial(kernel, (sections, seqs, tps, chunks)),...  96.2 us

profile of v3, /device:TPU:25, one launch (start us, length us, event | category | flops | bytes accessed | tf_op | source)
XLA Modules:
  0.0 97.9 jit_solution(9962594898518583425)
XLA Ops:
  0.0 96.2 %shard_map.100 = bf16[1,128,1024]{2,1,0:T(8,128)(2,1)} custom-call(bf16[128,1024]{1,0:T(8,128)(2,1)} %text_hbm.1, bf16[16,8192]{1,0:T(8,128)(2,1)} %img.1, s32[16]{0:T(128)} %target_hbm.1, bf16[1,1024]{1,0:T(2,128)(2,1)} %gain_hbm.1, bf16[8192,128]{1,0:T(8,128)(2,1)} %bitcast.5, bf16[1,128]{1,0:T(2,128)(2,1)} %q_bias_hbm.1, bf16[8192,256]{1,0:T(8,128)(2,1)} %bitcast.4, ...), custom_call_target="tpu_custom_call" | custom-call | tf_op jit(solution)/shard_map/pallas_call | solution.py:478
  96.2 1.7 %copy.12 = bf16[1,128,1024]{2,1,0:T(8,128)(2,1)} copy(bf16[1,128,1024]{2,1,0:T(8,128)(2,1)} %shard_map.100) | data formatting | bytes 524288

commit v4 on v2

--- a/solution.py
+++ b/solution.py
@@ -54,6 +54,8 @@
     w_out,
     rows,
     ctx,
+    part_out,
+    part_in,
     images,
     marks,
     gains,
@@ -62,8 +64,10 @@
     z_recv,
     far_send,
     far_recv,
-    fwd_send,
-    fwd_recv,
+    part_send,
+    part_recv,
+    w_send,
+    w_recv,
     ctx_send,
     ctx_recv,
     gain_send,
@@ -81,6 +85,9 @@
     me = my_s * tps + my_t
     mate = {"seq": my_s, "tp": my_t + 1 - 2 * lax.rem(my_t, 2)}
     mate_t = mate["tp"]
+    pairs = tps // 2
+    half = seqs * pairs
+    own = my_s * pairs + lax.div(my_t, 2)
     toks = text_hbm.shape[0] // MICRO
     width = text_hbm.shape[1]
     cw = width // chunks
@@ -125,20 +132,29 @@
         pltpu.make_async_copy(text_hbm, text, load_sem.at[3]),
     ]
     loads = [
-        pltpu.make_async_copy(q_hbm, w_all.at[:, pl.ds(0, hd)], load_sem.at[4]),
-        pltpu.make_async_copy(kv_hbm, w_all.at[:, pl.ds(hd, 2 * hd)], load_sem.at[5]),
-        pltpu.make_async_copy(q_bias_hbm, q_bias, load_sem.at[6]),
-        pltpu.make_async_copy(kv_bias_hbm, kv_bias, load_sem.at[7]),
-        pltpu.make_async_copy(table_hbm, table, load_sem.at[8]),
-        pltpu.make_async_copy(out_hbm, w_out, load_sem.at[9]),
+        pltpu.make_async_copy(q_bias_hbm, q_bias, load_sem.at[4]),
+        pltpu.make_async_copy(kv_bias_hbm, kv_bias, load_sem.at[5]),
+        pltpu.make_async_copy(table_hbm, table, load_sem.at[6]),
+        pltpu.make_async_copy(out_hbm, w_out, load_sem.at[7]),
     ]
-    for load in early + loads:
+    weights = []
+    for k in range(half):
+        p = lax.div(k, pairs) * tps + lax.rem(k, pairs) * 2 + lax.rem(my_t, 2)
+        at = pl.ds(pl.multiple_of(p * width, width), width)
+        to = pl.ds(k * width, width)
+        weights += [
+            pltpu.make_async_copy(q_hbm.at[at, :], w_all.at[to, pl.ds(0, hd)], load_sem.at[8 + 2 * k]),
+            pltpu.make_async_copy(
+                kv_hbm.at[at, :], w_all.at[to, pl.ds(hd, 2 * hd)], load_sem.at[9 + 2 * k]
+            ),
+        ]
+    for load in early + weights + loads:
         load.start()
     for load in early:
         load.wait()
 
     for j in range(width // LANES):
-        gains[me, j : j + 1, :] = gain[0:1, j * LANES : (j + 1) * LANES].astype(jnp.float32)
+        gains[own, j : j + 1, :] = gain[0:1, j * LANES : (j + 1) * LANES].astype(jnp.float32)
     lane = lax.broadcasted_iota(jnp.int32, (8, LANES), 1)
     row = lax.broadcasted_iota(jnp.int32, (8, LANES), 0)
     tile = jnp.full((8, LANES), -1, jnp.int32)
@@ -167,10 +183,34 @@
         )
 
     def gain_copy(i):
-        s, t = at_offset(*offsets[i])
+        s, t = at_offset(*far[i])
         return remote(
-            gains.at[me], gains.at[me], gain_send.at[i], gain_recv.at[i], {"seq": s, "tp": t}
-        )
+            gains.at[own], gains.at[own], gain_send.at[i], gain_recv.at[i], {"seq": s, "tp": t}
+        )
+
+    def weight_copies():
+        copies = []
+        for k in range(half):
+            p = lax.div(k, pairs) * tps + lax.rem(k, pairs) * 2 + lax.rem(mate_t, 2)
+            at = pl.ds(pl.multiple_of(p * width, width), width)
+            to = pl.ds(k * width, width)
+            copies += [
+                remote(
+                    q_hbm.at[at, :],
+                    w_all.at[to, pl.ds(3 * hd, hd)],
+                    w_send.at[2 * k],
+                    w_recv.at[2 * k],
+                    mate,
+                ),
+                remote(
+                    kv_hbm.at[at, :],
+                    w_all.at[to, pl.ds(4 * hd, 2 * hd)],
+                    w_send.at[2 * k + 1],
+                    w_recv.at[2 * k + 1],
+                    mate,
+                ),
+            ]
+        return copies
 
     def source(i):
         s, t = at_offset(*offsets[i], sign=-1)
@@ -182,8 +222,10 @@
             for copy in img_copy(i):
                 copy.start()
 
-    for i in range(len(offsets)):
+    for i in range(len(far)):
         gain_copy(i).start()
+    for copy in weight_copies():
+        copy.start()
 
     per_mb = members // MICRO
     position = lax.broadcasted_iota(jnp.int32, (toks, slots), 0)
@@ -207,7 +249,7 @@
         placed = jnp.dot(match.astype(jnp.bfloat16), stack, preferred_element_type=jnp.float32)
         is_image = jnp.max(match, axis=1, keepdims=True) > 0.5
         plain = text[m * toks : (m + 1) * toks, :].astype(jnp.float32)
-        rows[m, me] = jnp.where(is_image, placed, plain).astype(jnp.bfloat16)
+        rows[m, own] = jnp.where(is_image, placed, plain).astype(jnp.bfloat16)
 
     @pl.when(is_first)
     def _():
@@ -224,52 +266,22 @@
     def z_copy(m, c):
         return remote(
             out.at[0, pl.ds(m * toks, toks), cols_of(c)],
-            rows.at[m, me, :, cols_of(c)],
+            rows.at[m, own, :, cols_of(c)],
             z_send.at[m, c],
             z_recv.at[m, c],
             {"section": lax.rem(sec + 1, sections)},
         )
 
-    relayed = seqs == 2 and tps == 4 and chunks == 2
-    across = far.index((0, 2)) if relayed else None
-    along = far.index((1, 0)) if relayed else None
-    corner = far.index((1, 2)) if relayed else None
-
-    def direct(i):
-        return not relayed or i != corner
-
-    def relay(m, c):
-        got, to = (across, along) if c == 0 else (along, across)
-        s, t = at_offset(*far[to])
-        ref = rows.at[m, far_piece(got), :, cols_of(c)]
-        return remote(
-            ref,
-            ref,
-            far_send.at[m, c, corner],
-            far_recv.at[m, c, corner],
-            {"seq": s, "tp": t},
-        )
-
     def own_to(m, c, i):
         s, t = at_offset(*far[i])
-        ref = rows.at[m, me, :, cols_of(c)]
+        ref = rows.at[m, own, :, cols_of(c)]
         return remote(
             ref, ref, far_send.at[m, c, i], far_recv.at[m, c, i], {"seq": s, "tp": t}
         )
 
-    def far_piece(i):
+    def far_block(i):
         s, t = at_offset(*far[i], sign=-1)
-        return s * tps + t
-
-    def to_mate(m, c, i):
-        piece = me if i == 0 else far_piece(i - 1)
-        ref = rows.at[m, piece, :, cols_of(c)]
-        return remote(ref, ref, fwd_send.at[m, c, i], fwd_recv.at[m, c, i], mate)
-
-    def mate_piece(i):
-        ds, dt = (0, 0) if i == 0 else far[i - 1]
-        s, t = at_offset(ds, dt, sign=-1, base_t=mate_t)
-        return s * tps + t
+        return s * pairs + lax.div(t, 2)
 
     def launch(m):
         for c in range(chunks):
@@ -279,68 +291,49 @@
                 z_copy(m, c).wait_recv()
 
             for i in range(len(far)):
-                if direct(i):
-                    own_to(m, c, i).start()
-            to_mate(m, c, 0).start()
-
-    def piece_step(m, p, c, carry):
+                own_to(m, c, i).start()
+
+    def block_step(m, k, c, carry):
         total, squares = carry
-        piece = rows[m, p, :, c * cw : (c + 1) * cw].astype(jnp.float32)
+        piece = rows[m, k, :, c * cw : (c + 1) * cw].astype(jnp.float32)
         first = c * cw // LANES
         scale = jnp.concatenate(
-            [gains[p, pl.ds(first + j, 1), :] for j in range(cw // LANES)], axis=1
+            [gains[k, pl.ds(first + j, 1), :] for j in range(cw // LANES)], axis=1
         )
         for j in range(cw // LANES):
             part = piece[:, j * LANES : (j + 1) * LANES]
             squares = squares + part * part
-        weight = w_all[pl.ds(pl.multiple_of(p * width + c * cw, cw), cw), :]
+        weight = w_all[pl.ds(pl.multiple_of(k * width + c * cw, cw), cw), :]
         total = total + jnp.dot(
             (piece * scale).astype(jnp.bfloat16), weight, preferred_element_type=jnp.float32
         )
         return total, squares
 
-    def take_far(m, c, i, carry):
-        p = far_piece(i)
-        ref = rows.at[m, p, :, cols_of(c)]
-        remote(ref, ref, far_send.at[m, c, i], far_recv.at[m, c, i], mate).wait_recv()
-        if relayed and i == (across if c == 0 else along):
-            relay(m, c).start()
-        to_mate(m, c, i + 1).start()
-        return piece_step(m, p, c, carry)
-
-    def take_mate(m, c, i, carry):
-        p = mate_piece(i)
-        ref = rows.at[m, p, :, cols_of(c)]
-        remote(ref, ref, fwd_send.at[m, c, i], fwd_recv.at[m, c, i], mate).wait_recv()
-        return piece_step(m, p, c, carry)
-
-    def project_near(m):
+    def part_copy(m):
+        return remote(part_out.at[m], part_in.at[m], part_send.at[m], part_recv.at[m], mate)
+
+    def project(m):
         carry = (
-            jnp.zeros((toks, 3 * hd), jnp.float32),
+            jnp.zeros((toks, 6 * hd), jnp.float32),
             jnp.zeros((toks, LANES), jnp.float32),
         )
         for c in range(chunks):
-            carry = piece_step(m, me, c, carry)
+            carry = block_step(m, own, c, carry)
         for c in range(chunks):
-            carry = take_mate(m, c, 0, carry)
-        return carry
-
-    def project_far(m, carry):
-        late = [i for i in range(len(far)) if not direct(i)]
-        soon = [i for i in range(len(far)) if direct(i)]
-        for group in (soon, late):
-            for c in range(chunks):
-                order = group if c == 0 else group[::-1]
-                for i in order:
-                    carry = take_far(m, c, i, carry)
-                if group is late:
-                    continue
-                for i in order:
-                    carry = take_mate(m, c, i + 1, carry)
-        for c in range(chunks):
-            for i in late:
-                carry = take_mate(m, c, i + 1, carry)
-        return carry
+            for i in range(len(far)):
+                k = far_block(i)
+                ref = rows.at[m, k, :, cols_of(c)]
+                remote(
+                    ref, ref, far_send.at[m, c, i], far_recv.at[m, c, i], mate
+                ).wait_recv()
+                carry = block_step(m, k, c, carry)
+        total, squares = carry
+        part_out[m, :, : 3 * hd] = total[:, 3 * hd :]
+        part_out[m, :, 3 * hd :] = squares
+        part_copy(m).start()
+        part_copy(m).wait_recv()
+        total = total[:, : 3 * hd] + part_in[m, :, : 3 * hd]
+        return total, squares + part_in[m, :, 3 * hd :]
 
     def ctx_copy(m, i):
         s, t = at_offset(*offsets[i])
@@ -380,7 +373,7 @@
             update = jnp.dot(
                 ctx[m], w_out[:, c * cw : (c + 1) * cw], preferred_element_type=jnp.float32
             )
-            before = rows[m, me, :, c * cw : (c + 1) * cw].astype(jnp.float32)
+            before = rows[m, own, :, c * cw : (c + 1) * cw].astype(jnp.float32)
             out[0, m * toks : (m + 1) * toks, c * cw : (c + 1) * cw] = (before + update).astype(
                 jnp.bfloat16
             )
@@ -390,21 +383,23 @@
                 z_copy(m, c).start()
 
     launch(0)
-    for i in range(len(offsets)):
-        p = source(i)
+    for i in range(len(far)):
+        k = far_block(i)
         remote(
-            gains.at[p], gains.at[p], gain_send.at[i], gain_recv.at[i], mate
+            gains.at[k], gains.at[k], gain_send.at[i], gain_recv.at[i], mate
         ).wait_recv()
-    loads[0].wait()
-    loads[1].wait()
 
     @pl.when(is_first)
     def _():
         for m in range(1, MICRO):
             embed(m)
 
-    carry = project_far(0, project_near(0))
-    for load in loads[2:]:
+    for load in weights:
+        load.wait()
+    for copy in weight_copies():
+        copy.wait_recv()
+    carry = project(0)
+    for load in loads:
         load.wait()
     for m in range(MICRO):
         if m + 1 < MICRO:
@@ -420,20 +415,17 @@
             def _():
                 launch(m + 1)
 
-            carry = project_near(m + 1)
         finish(m)
         if m + 1 < MICRO:
-            carry = project_far(m + 1, carry)
-
+            carry = project(m + 1)
+
+    for copy in weight_copies():
+        copy.wait_send()
     for m in range(MICRO):
+        part_copy(m).wait_send()
         for c in range(chunks):
             for i in range(len(far)):
-                if direct(i):
-                    own_to(m, c, i).wait_send()
-            if relayed:
-                relay(m, c).wait_send()
-            for i in range(len(far) + 1):
-                to_mate(m, c, i).wait_send()
+                own_to(m, c, i).wait_send()
 
             @pl.when(sec < sections - 1)
             def _():
@@ -441,7 +433,7 @@
 
         for i in range(len(offsets)):
             ctx_copy(m, i).wait_send()
-    for i in range(len(offsets)):
+    for i in range(len(far)):
         gain_copy(i).wait_send()
 
     @pl.when(is_first)
@@ -472,7 +464,8 @@
     features = width * members
     cosine, signed_sine = tables(tok_count, head_size)
     others = members - 1
-    far = seqs * tps // 2 - 1
+    half = members // 2
+    far = half - 1
     vmem = pl.BlockSpec(memory_space=pltpu.VMEM)
     hbm = pl.BlockSpec(memory_space=pltpu.HBM)
     dma = pltpu.SemaphoreType.DMA
@@ -489,24 +482,28 @@
             pltpu.VMEM(q_bias.shape, bf16),
             pltpu.VMEM(kv_bias.shape[1:], bf16),
             pltpu.VMEM((2, tok_count, head_size), jnp.float32),
-            pltpu.VMEM((features, 3 * head_size), bf16),
+            pltpu.VMEM((half * width, 6 * head_size), bf16),
             pltpu.VMEM((members * head_size, width), bf16),
-            pltpu.VMEM((MICRO, members, tok_count, width), bf16),
+            pltpu.VMEM((MICRO, half, tok_count, width), bf16),
             pltpu.VMEM((MICRO, tok_count, members * head_size), bf16),
+            pltpu.VMEM((MICRO, tok_count, 3 * head_size + LANES), jnp.float32),
+            pltpu.VMEM((MICRO, tok_count, 3 * head_size + LANES), jnp.float32),
             pltpu.VMEM((members, image_rows.shape[0], width), bf16),
             pltpu.VMEM((members, 8, LANES), jnp.int32),
-            pltpu.VMEM((members, 8, LANES), jnp.float32),
-            dma((10,)),
+            pltpu.VMEM((half, 8, LANES), jnp.float32),
+            dma((8 + 2 * half,)),
             dma((MICRO, chunks)),
             dma((MICRO, chunks)),
             dma((MICRO, chunks, far)),
             dma((MICRO, chunks, far)),
-            dma((MICRO, chunks, far + 1)),
-            dma((MICRO, chunks, far + 1)),
+            dma((MICRO,)),
+            dma((MICRO,)),
+            dma((2 * half,)),
+            dma((2 * half,)),
             dma((MICRO, others)),
             dma((MICRO, others)),
-            dma((others,)),
-            dma((others,)),
+            dma((far,)),
+            dma((far,)),
             dma((others,)),
             dma((members,)),
             dma((others,)),

time: 94.6 us -> 91.1 us (0.963)
  Pallas kernels: 92.8 us -> 89.3 us
    pallas_call x1, Pallas kernels: 92.8 us -> 89.3 us  [per_device(): pl.pallas_call(functools.partial(kernel, (sections, seqs, tps, chunks)),...]
where the time goes in v4:
time: 91.1 us; the launch traced here: 91 us
  Pallas kernels  89.3 us (98%)
  local copies, waits for them, and re-layouts  1.67 us (2%)
    pallas_call x1, Pallas kernels, per_device(): pl.pallas_call(functools.partial(kernel, (sections, seqs, tps, chunks)),...  89.3 us

profile of v4, /device:TPU:25, one launch (start us, length us, event | category | flops | bytes accessed | tf_op | source)
XLA Modules:
  0.0 91.0 jit_solution(12018394143086587352)
XLA Ops:
  0.0 89.3 %shard_map.100 = bf16[1,128,1024]{2,1,0:T(8,128)(2,1)} custom-call(bf16[128,1024]{1,0:T(8,128)(2,1)} %text_hbm.1, bf16[16,8192]{1,0:T(8,128)(2,1)} %img.1, s32[16]{0:T(128)} %target_hbm.1, bf16[1,1024]{1,0:T(2,128)(2,1)} %gain_hbm.1, bf16[8192,128]{1,0:T(8,128)(2,1)} %bitcast.5, bf16[1,128]{1,0:T(2,128)(2,1)} %q_bias_hbm.1, bf16[8192,256]{1,0:T(8,128)(2,1)} %bitcast.4, ...), custom_call_target="tpu_custom_call" | custom-call | tf_op jit(solution)/shard_map/pallas_call | solution.py:473
  89.3 1.7 %copy.12 = bf16[1,128,1024]{2,1,0:T(8,128)(2,1)} copy(bf16[1,128,1024]{2,1,0:T(8,128)(2,1)} %shard_map.100) | data formatting | bytes 524288

commit v5 on v4

--- a/solution.py
+++ b/solution.py
@@ -312,28 +312,36 @@
     def part_copy(m):
         return remote(part_out.at[m], part_in.at[m], part_send.at[m], part_recv.at[m], mate)
 
-    def project(m):
+    def take(m, c, carry):
+        for i in range(len(far)):
+            k = far_block(i)
+            ref = rows.at[m, k, :, cols_of(c)]
+            remote(ref, ref, far_send.at[m, c, i], far_recv.at[m, c, i], mate).wait_recv()
+            carry = block_step(m, k, c, carry)
+        return carry
+
+    def project_first(m):
         carry = (
             jnp.zeros((toks, 6 * hd), jnp.float32),
             jnp.zeros((toks, LANES), jnp.float32),
         )
         for c in range(chunks):
             carry = block_step(m, own, c, carry)
-        for c in range(chunks):
-            for i in range(len(far)):
-                k = far_block(i)
-                ref = rows.at[m, k, :, cols_of(c)]
-                remote(
-                    ref, ref, far_send.at[m, c, i], far_recv.at[m, c, i], mate
-                ).wait_recv()
-                carry = block_step(m, k, c, carry)
+        return take(m, 0, carry)
+
+    def project_rest(m, carry):
+        for c in range(1, chunks):
+            carry = take(m, c, carry)
         total, squares = carry
         part_out[m, :, : 3 * hd] = total[:, 3 * hd :]
         part_out[m, :, 3 * hd :] = squares
         part_copy(m).start()
+        return total[:, : 3 * hd], squares
+
+    def combine(m, carry):
+        total, squares = carry
         part_copy(m).wait_recv()
-        total = total[:, : 3 * hd] + part_in[m, :, : 3 * hd]
-        return total, squares + part_in[m, :, 3 * hd :]
+        return total + part_in[m, :, : 3 * hd], squares + part_in[m, :, 3 * hd :]
 
     def ctx_copy(m, i):
         s, t = at_offset(*offsets[i])
@@ -393,31 +401,27 @@
     def _():
         for m in range(1, MICRO):
             embed(m)
+            launch(m)
 
     for load in weights:
         load.wait()
     for copy in weight_copies():
         copy.wait_recv()
-    carry = project(0)
+    carry = project_first(0)
     for load in loads:
         load.wait()
     for m in range(MICRO):
-        if m + 1 < MICRO:
-
-            @pl.when(is_first)
-            def _():
-                launch(m + 1)
-
-        attend(m, carry)
+        carry = project_rest(m, carry)
         if m + 1 < MICRO:
 
             @pl.when(sec > 0)
             def _():
                 launch(m + 1)
 
+        attend(m, combine(m, carry))
+        if m + 1 < MICRO:
+            carry = project_first(m + 1)
         finish(m)
-        if m + 1 < MICRO:
-            carry = project(m + 1)
 
     for copy in weight_copies():
         copy.wait_send()

time: 91.1 us -> 92.2 us (1.012)
  Pallas kernels: 89.3 us -> 90.4 us
    pallas_call x1, Pallas kernels: 89.3 us -> 90.4 us  [per_device(): pl.pallas_call(functools.partial(kernel, (sections, seqs, tps, chunks)),...]
where the time goes in v5:
time: 92.2 us; the launch traced here: 92.1 us
  Pallas kernels  90.4 us (98%)
  local copies, waits for them, and re-layouts  1.67 us (2%)
    pallas_call x1, Pallas kernels, per_device(): pl.pallas_call(functools.partial(kernel, (sections, seqs, tps, chunks)),...  90.4 us

profile of v5, /device:TPU:25, one launch (start us, length us, event | category | flops | bytes accessed | tf_op | source)
XLA Modules:
  0.0 92.1 jit_solution(9545478772815525472)
XLA Ops:
  0.0 90.4 %shard_map.100 = bf16[1,128,1024]{2,1,0:T(8,128)(2,1)} custom-call(bf16[128,1024]{1,0:T(8,128)(2,1)} %text_hbm.1, bf16[16,8192]{1,0:T(8,128)(2,1)} %img.1, s32[16]{0:T(128)} %target_hbm.1, bf16[1,1024]{1,0:T(2,128)(2,1)} %gain_hbm.1, bf16[8192,128]{1,0:T(8,128)(2,1)} %bitcast.5, bf16[1,128]{1,0:T(2,128)(2,1)} %q_bias_hbm.1, bf16[8192,256]{1,0:T(8,128)(2,1)} %bitcast.4, ...), custom_call_target="tpu_custom_call" | custom-call | tf_op jit(solution)/shard_map/pallas_call | solution.py:477
  90.4 1.7 %copy.12 = bf16[1,128,1024]{2,1,0:T(8,128)(2,1)} copy(bf16[1,128,1024]{2,1,0:T(8,128)(2,1)} %shard_map.100) | data formatting | bytes 524288

commit v6 on v5

--- a/solution.py
+++ b/solution.py
@@ -412,13 +412,13 @@
         load.wait()
     for m in range(MICRO):
         carry = project_rest(m, carry)
+        attend(m, combine(m, carry))
         if m + 1 < MICRO:
 
             @pl.when(sec > 0)
             def _():
                 launch(m + 1)
 
-        attend(m, combine(m, carry))
         if m + 1 < MICRO:
             carry = project_first(m + 1)
         finish(m)
@@ -464,7 +464,7 @@
     tok_count = text_rows.shape[0] // MICRO
     width = text_rows.shape[1]
     head_size = q_weight.shape[2]
-    chunks = 2 if width >= 512 else 1
+    chunks = max(1, width // 256)
     features = width * members
     cosine, signed_sine = tables(tok_count, head_size)
     others = members - 1

time: 92.2 us -> 87.8 us (0.952)
  Pallas kernels: 90.4 us -> 86 us
    pallas_call x1, Pallas kernels: 90.4 us -> 86 us  [per_device(): pl.pallas_call(functools.partial(kernel, (sections, seqs, tps, chunks)),...]
where the time goes in v6:
time: 87.8 us; the launch traced here: 87.7 us
  Pallas kernels  86 us (98%)
  local copies, waits for them, and re-layouts  1.67 us (2%)
    pallas_call x1, Pallas kernels, per_device(): pl.pallas_call(functools.partial(kernel, (sections, seqs, tps, chunks)),...  86 us

profile of v6, /device:TPU:25, one launch (start us, length us, event | category | flops | bytes accessed | tf_op | source)
XLA Modules:
  0.0 87.7 jit_solution(8058604524330888119)
XLA Ops:
  0.0 86.0 %shard_map.100 = bf16[1,128,1024]{2,1,0:T(8,128)(2,1)} custom-call(bf16[128,1024]{1,0:T(8,128)(2,1)} %text_hbm.1, bf16[16,8192]{1,0:T(8,128)(2,1)} %img.1, s32[16]{0:T(128)} %target_hbm.1, bf16[1,1024]{1,0:T(2,128)(2,1)} %gain_hbm.1, bf16[8192,128]{1,0:T(8,128)(2,1)} %bitcast.5, bf16[1,128]{1,0:T(2,128)(2,1)} %q_bias_hbm.1, bf16[8192,256]{1,0:T(8,128)(2,1)} %bitcast.4, ...), custom_call_target="tpu_custom_call" | custom-call | tf_op jit(solution)/shard_map/pallas_call | solution.py:477
  86.0 1.7 %copy.12 = bf16[1,128,1024]{2,1,0:T(8,128)(2,1)} copy(bf16[1,128,1024]{2,1,0:T(8,128)(2,1)} %shard_map.100) | data formatting | bytes 524288

commit v7 on v6

--- a/solution.py
+++ b/solution.py
@@ -188,29 +188,30 @@
             gains.at[own], gains.at[own], gain_send.at[i], gain_recv.at[i], {"seq": s, "tp": t}
         )
 
-    def weight_copies():
-        copies = []
-        for k in range(half):
-            p = lax.div(k, pairs) * tps + lax.rem(k, pairs) * 2 + lax.rem(mate_t, 2)
-            at = pl.ds(pl.multiple_of(p * width, width), width)
-            to = pl.ds(k * width, width)
-            copies += [
-                remote(
-                    q_hbm.at[at, :],
-                    w_all.at[to, pl.ds(3 * hd, hd)],
-                    w_send.at[2 * k],
-                    w_recv.at[2 * k],
-                    mate,
-                ),
-                remote(
-                    kv_hbm.at[at, :],
-                    w_all.at[to, pl.ds(4 * hd, 2 * hd)],
-                    w_send.at[2 * k + 1],
-                    w_recv.at[2 * k + 1],
-                    mate,
-                ),
-            ]
-        return copies
+    def weight_pair(k):
+        p = lax.div(k, pairs) * tps + lax.rem(k, pairs) * 2 + lax.rem(mate_t, 2)
+        at = pl.ds(pl.multiple_of(p * width, width), width)
+        to = pl.ds(pl.multiple_of(k * width, width), width)
+        return (
+            remote(
+                q_hbm.at[at, :],
+                w_all.at[to, pl.ds(3 * hd, hd)],
+                w_send.at[2 * k],
+                w_recv.at[2 * k],
+                mate,
+            ),
+            remote(
+                kv_hbm.at[at, :],
+                w_all.at[to, pl.ds(4 * hd, 2 * hd)],
+                w_send.at[2 * k + 1],
+                w_recv.at[2 * k + 1],
+                mate,
+            ),
+        )
+
+    def weight_wait(k):
+        for copy in weight_pair(k):
+            copy.wait_recv()
 
     def source(i):
         s, t = at_offset(*offsets[i], sign=-1)
@@ -224,8 +225,9 @@
 
     for i in range(len(far)):
         gain_copy(i).start()
-    for copy in weight_copies():
-        copy.start()
+    for j in range(half):
+        for copy in weight_pair(lax.rem(own + j, half)):
+            copy.start()
 
     per_mb = members // MICRO
     position = lax.broadcasted_iota(jnp.int32, (toks, slots), 0)
@@ -317,6 +319,8 @@
             k = far_block(i)
             ref = rows.at[m, k, :, cols_of(c)]
             remote(ref, ref, far_send.at[m, c, i], far_recv.at[m, c, i], mate).wait_recv()
+            if m == 0 and c == 0:
+                weight_wait(k)
             carry = block_step(m, k, c, carry)
         return carry
 
@@ -325,6 +329,8 @@
             jnp.zeros((toks, 6 * hd), jnp.float32),
             jnp.zeros((toks, LANES), jnp.float32),
         )
+        if m == 0:
+            weight_wait(own)
         for c in range(chunks):
             carry = block_step(m, own, c, carry)
         return take(m, 0, carry)
@@ -405,8 +411,6 @@
 
     for load in weights:
         load.wait()
-    for copy in weight_copies():
-        copy.wait_recv()
     carry = project_first(0)
     for load in loads:
         load.wait()
@@ -423,8 +427,9 @@
             carry = project_first(m + 1)
         finish(m)
 
-    for copy in weight_copies():
-        copy.wait_send()
+    for k in range(half):
+        for copy in weight_pair(k):
+            copy.wait_send()
     for m in range(MICRO):
         part_copy(m).wait_send()
         for c in range(chunks):

time: 87.8 us -> 87.8 us (level)
  no operation moved by 1% of the time
where the time goes in v7:
time: 87.8 us; the launch traced here: 87.7 us
  Pallas kernels  86 us (98%)
  local copies, waits for them, and re-layouts  1.67 us (2%)
    pallas_call x1, Pallas kernels, per_device(): pl.pallas_call(functools.partial(kernel, (sections, seqs, tps, chunks)),...  86 us

profile of v7, /device:TPU:25, one launch (start us, length us, event | category | flops | bytes accessed | tf_op | source)
XLA Modules:
  0.0 87.7 jit_solution(13645314970679019901)
XLA Ops:
  0.0 86.0 %shard_map.100 = bf16[1,128,1024]{2,1,0:T(8,128)(2,1)} custom-call(bf16[128,1024]{1,0:T(8,128)(2,1)} %text_hbm.1, bf16[16,8192]{1,0:T(8,128)(2,1)} %img.1, s32[16]{0:T(128)} %target_hbm.1, bf16[1,1024]{1,0:T(2,128)(2,1)} %gain_hbm.1, bf16[8192,128]{1,0:T(8,128)(2,1)} %bitcast.5, bf16[1,128]{1,0:T(2,128)(2,1)} %q_bias_hbm.1, bf16[8192,256]{1,0:T(8,128)(2,1)} %bitcast.4, ...), custom_call_target="tpu_custom_call" | custom-call | tf_op jit(solution)/shard_map/pallas_call | solution.py:482
  86.0 1.7 %copy.12 = bf16[1,128,1024]{2,1,0:T(8,128)(2,1)} copy(bf16[1,128,1024]{2,1,0:T(8,128)(2,1)} %shard_map.100) | data formatting | bytes 524288

commit v8 on v7

--- a/solution.py
+++ b/solution.py
@@ -225,9 +225,14 @@
 
     for i in range(len(far)):
         gain_copy(i).start()
-    for j in range(half):
-        for copy in weight_pair(lax.rem(own + j, half)):
-            copy.start()
+    def send_weights():
+        for j in range(half):
+            for copy in weight_pair(lax.rem(own + j, half)):
+                copy.start()
+
+    @pl.when(sec > 0)
+    def _():
+        send_weights()
 
     per_mb = members // MICRO
     position = lax.broadcasted_iota(jnp.int32, (toks, slots), 0)
@@ -397,17 +402,19 @@
                 z_copy(m, c).start()
 
     launch(0)
+
+    @pl.when(is_first)
+    def _():
+        send_weights()
+        for m in range(1, MICRO):
+            embed(m)
+            launch(m)
+
     for i in range(len(far)):
         k = far_block(i)
         remote(
             gains.at[k], gains.at[k], gain_send.at[i], gain_recv.at[i], mate
         ).wait_recv()
-
-    @pl.when(is_first)
-    def _():
-        for m in range(1, MICRO):
-            embed(m)
-            launch(m)
 
     for load in weights:
         load.wait()

time: 87.8 us -> 87.8 us (level)
  no operation moved by 1% of the time
where the time goes in v8:
time: 87.8 us; the launch traced here: 87.7 us
  Pallas kernels  86 us (98%)
  local copies, waits for them, and re-layouts  1.67 us (2%)
    pallas_call x1, Pallas kernels, per_device(): pl.pallas_call(functools.partial(kernel, (sections, seqs, tps, chunks)),...  86 us

profile of v8, /device:TPU:25, one launch (start us, length us, event | category | flops | bytes accessed | tf_op | source)
XLA Modules:
  0.0 87.7 jit_solution(9483927382378135929)
XLA Ops:
  0.0 86.0 %shard_map.100 = bf16[1,128,1024]{2,1,0:T(8,128)(2,1)} custom-call(bf16[128,1024]{1,0:T(8,128)(2,1)} %text_hbm.1, bf16[16,8192]{1,0:T(8,128)(2,1)} %img.1, s32[16]{0:T(128)} %target_hbm.1, bf16[1,1024]{1,0:T(2,128)(2,1)} %gain_hbm.1, bf16[8192,128]{1,0:T(8,128)(2,1)} %bitcast.5, bf16[1,128]{1,0:T(2,128)(2,1)} %q_bias_hbm.1, bf16[8192,256]{1,0:T(8,128)(2,1)} %bitcast.4, ...), custom_call_target="tpu_custom_call" | custom-call | tf_op jit(solution)/shard_map/pallas_call | solution.py:489
  86.0 1.7 %copy.12 = bf16[1,128,1024]{2,1,0:T(8,128)(2,1)} copy(bf16[1,128,1024]{2,1,0:T(8,128)(2,1)} %shard_map.100) | data formatting | bytes 524288
